TPU v7x, 512 devices: a whole 4x8x8 slice. The times are simulated.
512 devices in a mesh: pipe: 4 (over z_hi, core), seq: 32 (over y, x), dp: 4 (over z_lo).
Axes of the slice: x: 4, y: 8, z: 8 (z_hi: 2, z_lo: 4; z = z_hi * 4 + z_lo), core: 2. Of those that a mesh axis runs over, the one named last changes fastest.
Arguments:
- inputs: bfloat16 [4, 2, 2048, 4096], P('dp', None, 'seq'), may hold values from -40 to 40
- weights: bfloat16 [4, 32, 4, 128, 128], P(None, 'seq'), may hold values from -1 to 1, as said below
- gains: float32 [4, 4096], replicated, may hold values from 0.25 to 1.75
- doc_lengths: int32 [4, 2, 48], P('dp'), may hold values from 1 to 64, 2048 in all within a row
Outputs:
- weight_grads: float32 [4, 32, 4, 128, 128], P('pipe', 'seq')
Inputs may be any that keep to these rules, and one draw needn't show every extreme that they name: In each block weights[s, j, m] every entry is 0 or plus or minus one positive value of that block. `doc_lengths`: the lengths in each row sum to 2048 and are the documents of that micro-batch in order.
All inputs are finite; a program needn't handle non-finite values.
Results may differ from a plain program's by a relative error of at most 0.015.
Values may be sent and summed in bfloat16 or wider, within the bound.
A program may use at most 128 MiB of HBM per device.

v0:
```python
from functools import partial

import jax
import jax.numpy as jnp
from jax import lax
from jax.sharding import PartitionSpec as P

EPSILON = 1e-06


def from_behind(value, axis, steps):
    count = lax.axis_size(axis)
    first, last = (max(0, -steps), min(count, count - steps))
    return lax.ppermute(value, axis, [(source, source + steps) for source in range(first, last)])


def from_partner(block, axis, apart):
    count = lax.axis_size(axis)
    route = []
    for low in range(count):
        high = low | 1 << apart
        if high != low and high < count:
            route += [(low, high), (high, low)]
    return lax.ppermute(block, axis, route)


def mix(form, left, right):
    return jnp.einsum(form, left, right, preferred_element_type=jnp.float32)


def windowed(values, blocks, span):
    shaped = values.reshape((blocks, span) + values.shape[1:])
    earlier = jnp.concatenate([jnp.zeros_like(shaped[:1]), shaped[:-1]], axis=0)
    return jnp.concatenate([earlier, shaped], axis=1)


def unwindow(values, span):
    blocks = values.shape[0]
    inside = values[:, span:]
    later = jnp.concatenate([values[1:, :span], jnp.zeros_like(values[:1, :span])], axis=0)
    return (inside + later).reshape((blocks * span,) + values.shape[2:])


def doc_mask(lengths, total, span):
    ends = jnp.cumsum(lengths)
    places = jnp.arange(total, dtype=jnp.int32)
    owner = jnp.sum((ends[None, :] <= places[:, None]).astype(jnp.int32), axis=1)
    blocks = total // span
    owner_q = owner.reshape(blocks, span)
    owner_prev = jnp.concatenate([jnp.full((1, span), -1, jnp.int32), owner_q[:-1]], axis=0)
    owner_k = jnp.concatenate([owner_prev, owner_q], axis=1)
    row_place = jnp.arange(span, dtype=jnp.int32)[:, None]
    col_place = jnp.arange(2 * span, dtype=jnp.int32)[None, :]
    return (owner_q[:, :, None] == owner_k[:, None, :]) & (col_place <= row_place + span)[None]


def head_core(inputs_h, weights_h, allowed, span):
    tokens, heads, width = inputs_h.shape
    blocks = tokens // span
    query = mix("shc,hcd->shd", inputs_h, weights_h[:, 0])
    keys = mix("shc,hcd->shd", inputs_h, weights_h[:, 1])
    values = mix("shc,hcd->shd", inputs_h, weights_h[:, 2]).astype(jnp.bfloat16)
    query_scale = lax.rsqrt(jnp.mean(query * query, axis=-1, keepdims=True) + EPSILON)
    key_scale = lax.rsqrt(jnp.mean(keys * keys, axis=-1, keepdims=True) + EPSILON)
    query_blocks = (query * query_scale).astype(jnp.bfloat16).reshape(blocks, span, heads, width)
    key_window = windowed((keys * key_scale).astype(jnp.bfloat16), blocks, span)
    value_window = windowed(values, blocks, span)
    scores = mix("bqhd,bkhd->bhqk", query_blocks, key_window) * width ** (-0.5)
    raised = jnp.where(allowed[:, None], jnp.exp(scores), 0.0)
    attention = (raised / jnp.sum(raised, axis=-1, keepdims=True)).astype(jnp.bfloat16)
    mixed = (
        mix("bhqk,bkhd->bqhd", attention, value_window)
        .astype(jnp.bfloat16)
        .reshape(tokens, heads, width)
    )
    return (
        query,
        keys,
        query_scale,
        key_scale,
        query_blocks,
        key_window,
        value_window,
        attention,
        mixed,
    )


def head_back(inputs_h, weights_h, cached, branch_grad, span):
    (
        query,
        keys,
        query_scale,
        key_scale,
        query_blocks,
        key_window,
        value_window,
        attention,
        mixed,
    ) = cached
    tokens, heads, width = inputs_h.shape
    blocks = tokens // span
    grad_out = mix("shd,she->hde", mixed, branch_grad)
    grad_mixed = (
        mix("she,hde->shd", branch_grad, weights_h[:, 3])
        .astype(jnp.bfloat16)
        .reshape(blocks, span, heads, width)
    )
    grad_attention = mix("bqhd,bkhd->bhqk", grad_mixed, value_window)
    grad_values = unwindow(mix("bhqk,bqhd->bkhd", attention, grad_mixed), span).astype(jnp.bfloat16)
    chances = attention.astype(jnp.float32)
    grad_scores = (
        chances
        * (grad_attention - jnp.sum(grad_attention * chances, axis=-1, keepdims=True))
        * width ** (-0.5)
    ).astype(jnp.bfloat16)
    unit_query_grad = mix("bhqk,bkhd->bqhd", grad_scores, key_window).reshape(tokens, heads, width)
    unit_key_grad = unwindow(mix("bhqk,bqhd->bkhd", grad_scores, query_blocks), span)
    grad_query = (
        query_scale * unit_query_grad
        - query * query_scale**3 * jnp.mean(unit_query_grad * query, axis=-1, keepdims=True)
    ).astype(jnp.bfloat16)
    grad_keys = (
        key_scale * unit_key_grad
        - keys * key_scale**3 * jnp.mean(unit_key_grad * keys, axis=-1, keepdims=True)
    ).astype(jnp.bfloat16)
    grad_in = (
        mix("shd,hcd->shc", grad_query, weights_h[:, 0])
        + mix("shd,hcd->shc", grad_keys, weights_h[:, 1])
        + mix("shd,hcd->shc", grad_values, weights_h[:, 2])
    )
    grads = jnp.stack(
        [
            mix("shc,shd->hcd", inputs_h, grad_query),
            mix("shc,shd->hcd", inputs_h, grad_keys),
            mix("shc,shd->hcd", inputs_h, grad_values),
            grad_out,
        ],
        axis=1,
    )
    return (grad_in.astype(jnp.bfloat16), grads)


def head_layout(values):
    return lax.all_to_all(values, "seq", split_axis=1, concat_axis=0, tiled=True)


def token_layout(values):
    return lax.all_to_all(values, "seq", split_axis=0, concat_axis=1, tiled=True)


def feature_mean(partial_sums, width):
    return partial_sums / width


def normalize(state, gain_row, width):
    wide = state.astype(jnp.float32)
    scale = lax.rsqrt(feature_mean(jnp.sum(wide * wide, axis=-1, keepdims=True), width) + EPSILON)
    return ((wide * scale * gain_row).astype(jnp.bfloat16), scale)


def store_slot(stores, record, slot):
    return tuple(
        (
            lax.dynamic_update_index_in_dim(store, item, slot, 0)
            for store, item in zip(stores, record)
        )
    )


def read_slot(stores, slot):
    return tuple((lax.dynamic_index_in_dim(store, slot, 0, keepdims=False) for store in stores))


def forward_branch(operands, span, width):
    state, gain_row, weights_h, allowed, slot, stores = operands
    normed, scale = normalize(state, gain_row, width)
    inputs_h = head_layout(normed)
    heads = weights_h.shape[0]
    shaped = inputs_h.reshape(inputs_h.shape[0], heads, inputs_h.shape[1] // heads)
    cached = head_core(shaped, weights_h, allowed, span)
    branch = mix("shd,hde->she", cached[-1], weights_h[:, 3]).astype(jnp.bfloat16)
    branch = token_layout(branch.reshape(inputs_h.shape))
    stepped = (state.astype(jnp.float32) + branch.astype(jnp.float32)).astype(jnp.bfloat16)
    record = (state, inputs_h, scale) + tuple(cached)
    return (stepped, store_slot(stores, record, slot))


def forward_skip(operands, span, width):
    return (operands[0], operands[5])


def backward_branch(operands, span, width):
    cotangent, gain_row, weights_h, allowed, slot, stores = operands
    record = read_slot(stores, slot)
    state, inputs_h, scale = (record[0], record[1], record[2])
    cached = record[3:]
    heads = weights_h.shape[0]
    shaped = inputs_h.reshape(inputs_h.shape[0], heads, inputs_h.shape[1] // heads)
    branch_grad = head_layout(cotangent).reshape(shaped.shape)
    grad_h, grads = head_back(shaped, weights_h, cached, branch_grad, span)
    grad_normed = token_layout(grad_h.reshape(inputs_h.shape))
    wide = state.astype(jnp.float32)
    pulled = grad_normed.astype(jnp.float32) * gain_row
    along = feature_mean(jnp.sum(pulled * wide, axis=-1, keepdims=True), width)
    carried = scale * pulled - wide * scale**3 * along
    return ((cotangent.astype(jnp.float32) + carried).astype(jnp.bfloat16), grads)


def backward_skip(operands, span, width):
    return (operands[0], jnp.zeros(operands[2].shape, jnp.float32))


def blank_stores(rows, state_width, total, columns, heads, head_width, span):
    blocks = total // span
    shapes = [
        ((rows, state_width), jnp.bfloat16),
        ((total, columns), jnp.bfloat16),
        ((rows, 1), jnp.float32),
        ((total, heads, head_width), jnp.float32),
        ((total, heads, head_width), jnp.float32),
        ((total, heads, 1), jnp.float32),
        ((total, heads, 1), jnp.float32),
        ((blocks, span, heads, head_width), jnp.bfloat16),
        ((blocks, 2 * span, heads, head_width), jnp.bfloat16),
        ((blocks, 2 * span, heads, head_width), jnp.bfloat16),
        ((blocks, heads, span, 2 * span), jnp.bfloat16),
        ((total, heads, head_width), jnp.bfloat16),
    ]
    return tuple((jnp.zeros((2,) + shape, kind) for shape, kind in shapes))


def pass_along(state, direction):
    return from_behind(state, "pipe", direction)


def mirror_across(values, sections):
    for bit_place in range(sections.bit_length() - 1):
        values = from_partner(values.astype(jnp.bfloat16), "pipe", bit_place).astype(values.dtype)
    return values


def pick_section(array, index):
    return lax.dynamic_index_in_dim(array, index, 0, keepdims=False)


def local(inputs, weights, gains, doc_lengths):
    sections = lax.axis_size("pipe")
    place = lax.axis_index("pipe")
    tok_dev = inputs.shape[2]
    total = tok_dev * lax.axis_size("seq")
    span = min(tok_dev, total // 2)
    width = gains.shape[1]
    columns = width // lax.axis_size("seq")
    gain_down = pick_section(gains, place)
    gain_up = pick_section(gains, sections - 1 - place)
    down_state, up_state = (inputs[0, 0], inputs[0, 1])
    weights_down = pick_section(weights, place)
    weights_up = pick_section(weights, sections - 1 - place)
    mask_down = doc_mask(doc_lengths[0, 0], total, span)
    mask_up = doc_mask(doc_lengths[0, 1], total, span)
    heads = weights.shape[1]
    head_width = weights.shape[3]
    stores = blank_stores(
        down_state.shape[0], down_state.shape[1], total, columns, heads, head_width, span
    )
    run_forward = partial(forward_branch, span=span, width=width)
    skip_forward = partial(forward_skip, span=span, width=width)
    run_backward = partial(backward_branch, span=span, width=width)
    skip_backward = partial(backward_skip, span=span, width=width)

    def pick(use_down, first, second):
        return jnp.where(use_down, first, second)

    down_x, up_x = (down_state, up_state)
    for step in range(sections):
        use_down = place == step
        use_up = place == sections - 1 - step
        slot = jnp.where(use_down, 0, 1).astype(jnp.int32)
        operands = (
            pick(use_down, down_x, up_x),
            pick(use_down, gain_down, gain_up),
            pick(use_down, weights_down, weights_up),
            pick(use_down, mask_down, mask_up),
            slot,
            stores,
        )
        stepped, stores = lax.cond(use_down | use_up, run_forward, skip_forward, operands)
        down_x = jnp.where(use_down, stepped, down_x)
        up_x = jnp.where(use_up, stepped, up_x)
        if step < sections - 1:
            down_x = pass_along(down_x, 1)
            up_x = pass_along(up_x, -1)
    down_grad, up_grad = (down_x, up_x)
    own_grads = jnp.zeros(weights.shape[1:], jnp.float32)
    mirror_grads = jnp.zeros(weights.shape[1:], jnp.float32)
    for step in range(sections):
        use_down = place == sections - 1 - step
        use_up = place == step
        slot = jnp.where(use_down, 0, 1).astype(jnp.int32)
        operands = (
            pick(use_down, down_grad, up_grad),
            pick(use_down, gain_down, gain_up),
            pick(use_down, weights_down, weights_up),
            pick(use_down, mask_down, mask_up),
            slot,
            stores,
        )
        new_grad, part_grads = lax.cond(use_down | use_up, run_backward, skip_backward, operands)
        own_grads = own_grads + jnp.where(use_down, part_grads, 0.0)
        mirror_grads = mirror_grads + jnp.where(use_up, part_grads, 0.0)
        down_grad = jnp.where(use_down, new_grad, down_grad)
        up_grad = jnp.where(use_up, new_grad, up_grad)
        if step < sections - 1:
            down_grad = pass_along(down_grad, -1)
            up_grad = pass_along(up_grad, 1)
    own_sum, mirror_sum = (
        lax.psum(own_grads.astype(jnp.bfloat16), "dp").astype(jnp.float32),
        lax.psum(mirror_grads.astype(jnp.bfloat16), "dp").astype(jnp.float32),
    )
    summed = own_sum + mirror_across(mirror_sum, sections)
    return summed[None]


def solution(mesh):
    placed = (
        P("dp", None, "seq", None),
        P(None, "seq", None, None, None),
        P(),
        P("dp", None, None),
    )
    return jax.shard_map(
        local,
        mesh=mesh,
        in_specs=placed,
        out_specs=P("pipe", "seq", None, None, None),
        check_vma=False,
    )
```

profile of v0, /device:TPU:6, one launch (start us, length us, event | category | flops | bytes accessed | tf_op | source)
XLA Modules:
  0.0 671.4 jit_solution(5523687023002898590)
XLA Ops:
  12.9 60.3 %conditional.8 = (bf16[64,4096]{1,0:T(8,128)(2,1)S(1)}, bf16[2,64,4096]{2,1,0:T(8,128)(2,1)}, bf16[2,2048,128]{2,1,0:T(8,128)(2,1)S(1)}, f32[2,64,1]{1,2,0:T(1,1...) conditional(s32[]{:T(128)} %convert_element_type.707, ...), branch_computations={%region_4.5_spmd, %region_5.10_spmd} | conditional | flops 422324544 | bytes 90969320 | solution.py:288
  14.2 10.2 %all-to-all-start = ((bf16[64,32,128]{2,0,1:T(8,128)(2,1)}), bf16[64,32,128]{2,0,1:T(8,128)(2,1)S(1)}, u32[]{:S(2)}, u32[]{:S(2)}) async-start(bf16[64,32,128]{2,0,1:T(8,128)(2,1)} %copy_bitcast_fusion), calls=%async_computation | async-start | bytes 1048576 | tf_op jit(solution)/shard_map/cond/branch_1_fun/all_to_all | solution.py:145
  26.3 10.7 %all-to-all-done = bf16[64,32,128]{2,0,1:T(8,128)(2,1)S(1)} async-done(((bf16[64,32,128]{2,0,1:T(8,128)(2,1)}), bf16[64,32,128]{2,0,1:T(8,128)(2,1)S(1)}, u32[]{:S(2)}, u32[]{:S(2)}) %all-to-all-start) | async-done | bytes 524320 | tf_op jit(solution)/shard_map/cond/branch_1_fun/all_to_all | solution.py:145
  41.8 3.2 bitcast_dynamic-update-slice_fusion.4
  45.0 2.0 convolution_convert_fusion.2
  47.8 1.9 convolution_convert_fusion
  49.7 5.6 all-to-all-start.1
  55.3 1.8 broadcast.1084.clone
  57.1 2.2 bitcast_dynamic-update-slice_fusion.3
  59.3 1.8 broadcast.1084.clone.1
  73.2 2.3 bitcast_select_fusion
  76.8 3.8 collective-permute-start
  82.9 8.5 %conditional.9 = ((bf16[64,4096]{1,0:T(8,128)(2,1)S(1)}, bf16[2,64,4096]{2,1,0:T(8,128)(2,1)}, bf16[2,2048,128]{2,1,0:T(8,128)(2,1)S(1)}, f32[2,64,1]{1,2,0:T(1,...) conditional(s32[]{:T(128)} %convert_element_type.708, ...), branch_computations={%region_10.11_spmd, %region_11.16_spmd} | conditional | flops 421796160 | bytes 62377712 | solution.py:288
  91.3 2.3 broadcast_select_fusion.14
  94.9 52.8 %collective-permute-start.2 = (bf16[64,4096]{1,0:T(8,128)(2,1)}, bf16[64,4096]{1,0:T(8,128)(2,1)}, u32[]{:S(2)}, u32[]{:S(2)}) collective-permute-start(bf16[64,4096]{1,0:T(8,128)(2,1)} %get-tuple-element.797), channel_id=1, source_target_pairs={{0,128},{128,256},{256,384},{1,129},{129,257},{257,385},{2,130},{1... | collective-permute-start | bytes 1572872 | tf_op jit(solution)/shard_map/ppermute | solution.py:14
  148.9 2.3 broadcast_select_fusion.6
  152.4 71.4 %collective-permute-start.4 = (bf16[64,4096]{1,0:T(8,128)(2,1)}, bf16[64,4096]{1,0:T(8,128)(2,1)}, u32[]{:S(2)}, u32[]{:S(2)}) collective-permute-start(bf16[64,4096]{1,0:T(8,128)(2,1)} %get-tuple-element.795), channel_id=1, source_target_pairs={{0,128},{128,256},{256,384},{1,129},{129,257},{257,385},{2,130},{1... | collective-permute-start | bytes 1572872 | tf_op jit(solution)/shard_map/ppermute | solution.py:14
  224.9 52.2 %conditional.11 = ((bf16[64,4096]{1,0:T(8,128)(2,1)S(1)}, bf16[2,64,4096]{2,1,0:T(8,128)(2,1)}, bf16[2,2048,128]{2,1,0:T(8,128)(2,1)S(1)}, f32[2,64,1]{1,2,0:T(1...) conditional(s32[]{:T(128)} %convert_element_type.707, ...), branch_computations={%region_22.23_spmd, %region_23.28_spmd} | conditional | flops 421796160 | bytes 62377712 | solution.py:288
  225.7 1.8 copy_bitcast_fusion.3
  227.5 5.6 all-to-all-start.6
  235.2 10.5 %all-to-all-done.6 = bf16[64,32,128]{2,0,1:T(8,128)(2,1)S(1)} async-done(((bf16[64,32,128]{2,0,1:T(8,128)(2,1)}), bf16[64,32,128]{2,0,1:T(8,128)(2,1)S(1)}, u32[]{:S(2)}, u32[]{:S(2)}) %all-to-all-start.6) | async-done | bytes 524320 | tf_op jit(solution)/shard_map/cond/branch_1_fun/all_to_all | solution.py:145
  250.4 3.3 bitcast_dynamic-update-slice_fusion.22
  253.7 1.8 convolution_convert_fusion.11
  257.3 5.7 all-to-all-start.7
  263.2 3.2 bitcast_dynamic-update-slice_fusion.20
  269.5 6.2 all-to-all-done.7
  278.2 75.5 %conditional.12 = (bf16[64,4096]{1,0:T(8,128)(2,1)S(1)}, f32[1,4,128,128]{3,2,1,0:T(8,128)}) conditional(s32[]{:T(128)} %convert_element_type.707, bf16[64,4096]{1,0:T(8,128)(2,1)S(1)} %broadcast_select_fusion.16, (bf16[64,4096]{1,0:T(8,128)(2,1)S(1)}, s32[]{:T(128)}, f32[2,64,1]{1,2,0:T(1,128)}, f32[2,2048,1,1]{1,3,2,0:T(1,128)}, ...), branch_computations={%region_28.29_spmd, %region_29.34_spmd} | conditional | flops 818622848 | bytes 103325520 | solution.py:309
  279.2 6.4 all-to-all-start.8
  287.5 3.0 constant_dynamic-slice_fusion
  290.5 7.6 %all-to-all-done.8 = bf16[64,32,128]{2,0,1:T(8,128)(2,1)} async-done(((bf16[64,32,128]{2,0,1:T(8,128)(2,1)}), bf16[64,32,128]{2,0,1:T(8,128)(2,1)}, u32[]{:S(2)}, u32[]{:S(2)}) %all-to-all-start.8) | async-done | bytes 524320 | tf_op jit(solution)/shard_map/cond/branch_1_fun/all_to_all | solution.py:145
  298.1 2.1 fusion.146
  300.3 2.0 copy.109
  302.3 3.2 fusion.170
  305.5 1.8 convolution_bitcast_fusion
  307.4 3.8 convolution_bitcast_fusion.1
  311.1 4.2 fusion.166
  318.1 2.3 fusion.175
  327.0 2.3 fusion.176
  330.8 5.9 all-to-all-start.9
  342.5 7.0 %all-to-all-done.9 = bf16[32,64,128]{2,1,0:T(8,128)(2,1)} async-done(((bf16[32,64,128]{2,1,0:T(8,128)(2,1)}), bf16[32,64,128]{2,1,0:T(8,128)(2,1)}, u32[]{:S(2)}, u32[]{:S(2)}) %all-to-all-start.9) | async-done | bytes 524320 | tf_op jit(solution)/shard_map/cond/branch_1_fun/all_to_all | solution.py:149
  349.5 2.1 fusion.160
  357.8 2.3 collective-permute-done.6
  363.3 81.4 %collective-permute-start.9 = (bf16[64,4096]{1,0:T(8,128)(2,1)S(1)}, bf16[64,4096]{1,0:T(8,128)(2,1)S(1)}, u32[]{:S(2)}, u32[]{:S(2)}) collective-permute-start(bf16[64,4096]{1,0:T(8,128)(2,1)S(1)} %get-tuple-element.788), channel_id=1, source_target_pairs={{0,128},{128,256},{256,384},{1,129},{129,257},{257,385},{2,130},{1... | collective-permute-start | bytes 1572872 | tf_op jit(solution)/shard_map/ppermute | solution.py:14
  446.2 4.0 collective-permute-done.8
  451.3 5.3 conditional.14
  458.0 81.0 %collective-permute-start.11 = (bf16[64,4096]{1,0:T(8,128)(2,1)S(1)}, bf16[64,4096]{1,0:T(8,128)(2,1)S(1)}, u32[]{:S(2)}, u32[]{:S(2)}) collective-permute-start(bf16[64,4096]{1,0:T(8,128)(2,1)S(1)} %get-tuple-element.786), channel_id=1, source_target_pairs={{0,128},{128,256},{256,384},{1,129},{129,257},{257,385},{2,130},{1... | collective-permute-start | bytes 1572872 | tf_op jit(solution)/shard_map/ppermute | solution.py:14
  540.5 4.2 collective-permute-done.10
  544.7 45.0 %conditional.15 = (f32[1,4,128,128]{3,2,1,0:T(8,128)S(1)}) conditional(s32[]{:T(128)} %convert_element_type.707, () %tuple.74, (s32[]{:T(128)}, bf16[2,2048,128]{2,1,0:T(8,128)(2,1)S(1)}, f32[2,2048,1,1]{1,3,2,0:T(1,128)S(1)}, bf16[2,32,128,1,128]{4,2,1,3,0:T(8,128)(2,1)}, bf16[2,32,1,64,128]{4,3,1,2,0:T(8,128)(2,1)S(1)}, /*index=5*/pred[]{:T(512)}, ...), branch_computations={%region_46.47_spmd, %region_47.51_spmd} | conditional | flops 612839680 | bytes 79107488 | solution.py:309
  544.7 2.0 copy_bitcast_fusion.7
  546.7 5.6 all-to-all-start.14
  553.5 3.0 constant_dynamic-slice_fusion.15
  556.5 8.4 %all-to-all-done.14 = bf16[64,32,128]{2,0,1:T(8,128)(2,1)S(1)} async-done(((bf16[64,32,128]{2,0,1:T(8,128)(2,1)}), bf16[64,32,128]{2,0,1:T(8,128)(2,1)S(1)}, u32[]{:S(2)}, u32[]{:S(2)}) %all-to-all-start.14) | async-done | bytes 524320 | tf_op jit(solution)/shard_map/cond/branch_1_fun/all_to_all | solution.py:145
  567.3 2.0 fusion.396
  569.4 1.8 convolution_bitcast_fusion.18
  571.2 3.1 convolution_bitcast_fusion.19
  579.6 3.3 fusion.392
  584.5 2.7 convolution_bitcast_fusion.22
  587.2 2.5 convolution_bitcast_fusion.23
  589.8 1.9 add_convert_fusion.1
  591.7 53.7 %all-reduce.21.cloned.1.call-done = (bf16[1,4,128,128]{3,2,1,0:T(8,128)(2,1)}, bf16[1,4,128,128]{3,2,1,0:T(8,128)(2,1)}) async-done(((bf16[1,4,128,128]{3,2,1,0:T(8,128)(2,1)}, bf16[1,4,128,128]{3,2,1,0:T(8,128)(2,1)}), (bf16[1,4,128,128]{3,2,1,0:T(8,128)(2,1)}, bf16[1,4,128,128]{3,2,1,0:T(8,128)(2,1)})) %all-reduce.21.cloned.1.call-update) | async-done | bytes 262160 | tf_op jit(solution)/shard_map/psum | solution.py:319
  645.4 1.9 collective-permute-start.12
  648.8 5.3 collective-permute-start.13
  654.1 8.6 %collective-permute-done.13 = bf16[1,4,128,128]{3,2,1,0:T(8,128)(2,1)S(1)} collective-permute-done((bf16[1,4,128,128]{3,2,1,0:T(8,128)(2,1)S(1)}, bf16[1,4,128,128]{3,2,1,0:T(8,128)(2,1)S(1)}, u32[]{:S(2)}, u32[]{:S(2)}) %collective-permute-start.13) | collective-permute-done | bytes 131104 | tf_op jit(solution)/shard_map/ppermute | solution.py:24
  662.7 1.6 add_bitcast_fusion
  (300 shorter events, 96.7 us)
Async XLA Ops:
  6.5 5.7 copy-start.108
  6.5 638.8 %all-reduce.21.cloned.1.call-start = ((), (), s32[]{:S(2)}) async-start(), calls=%async_computation.15 | async-start | bytes 524288 | tf_op jit(solution)/shard_map/psum | solution.py:319
  13.2 23.9 %copy-start.85 = (bf16[1,4,128,128]{3,2,1,0:T(8,128)(2,1)S(1)}, bf16[1,4,128,128]{3,2,1,0:T(8,128)(2,1)}, u32[]{:S(2)}) copy-start(bf16[1,4,128,128]{3,2,1,0:T(8,128)(2,1)} %get-tuple-element.363) | copy-start | bytes 393220 | tf_op jit(solution)/shard_map/cond
  14.2 22.8 %all-to-all-start = ((bf16[64,32,128]{2,0,1:T(8,128)(2,1)}), bf16[64,32,128]{2,0,1:T(8,128)(2,1)S(1)}, u32[]{:S(2)}, u32[]{:S(2)}) async-start(bf16[64,32,128]{2,0,1:T(8,128)(2,1)} %copy_bitcast_fusion), calls=%async_computation | async-start | bytes 1048576 | tf_op jit(solution)/shard_map/cond/branch_1_fun/all_to_all | solution.py:145
  24.4 12.6 %copy-start.128 = (f32[2,64,1]{1,2,0:T(1,128)}, f32[2,64,1]{1,2,0:T(1,128)S(1)}, u32[]{:S(2)}) copy-start(f32[2,64,1]{1,2,0:T(1,128)S(1)} %constant_dynamic-update-slice_fusion.4) | copy-start | bytes 1540 | tf_op jit(solution)/shard_map/cond
  38.3 3.2 copy-start.6
  45.0 4.7 copy-start
  49.7 22.2 %all-to-all-start.1 = ((bf16[32,64,128]{2,1,0:T(8,128)(2,1)}), bf16[32,64,128]{2,1,0:T(8,128)(2,1)}, u32[]{:S(2)}, u32[]{:S(2)}) async-start(bf16[32,64,128]{2,1,0:T(8,128)(2,1)} %bitcast.1209), calls=%async_computation.1 | async-start | bytes 1048576 | tf_op jit(solution)/shard_map/cond/branch_1_fun/all_to_all | solution.py:149
  57.1 4.0 copy-start.83
  62.4 3.4 copy-start.71
  62.5 4.2 copy-start.2
  62.6 4.1 copy-start.90
  62.6 4.1 copy-start.99
  64.6 3.6 copy-start.7
  68.2 2.6 copy-start.5
  70.8 2.5 copy-start.3
  75.6 6.5 collective-permute-start.1
  76.8 5.2 collective-permute-start
  93.6 54.1 %collective-permute-start.3 = (bf16[64,4096]{1,0:T(8,128)(2,1)}, bf16[64,4096]{1,0:T(8,128)(2,1)S(1)}, u32[]{:S(2)}, u32[]{:S(2)}) collective-permute-start(bf16[64,4096]{1,0:T(8,128)(2,1)} %get-tuple-element.796), channel_id=1, source_target_pairs={{128,0},{256,128},{384,256},{129,1},{257,129},{385,257},{130,2},{2... | collective-permute-start | bytes 1572872 | tf_op jit(solution)/shard_map/ppermute | solution.py:14
  94.9 53.9 %collective-permute-start.2 = (bf16[64,4096]{1,0:T(8,128)(2,1)}, bf16[64,4096]{1,0:T(8,128)(2,1)}, u32[]{:S(2)}, u32[]{:S(2)}) collective-permute-start(bf16[64,4096]{1,0:T(8,128)(2,1)} %get-tuple-element.797), channel_id=1, source_target_pairs={{0,128},{128,256},{256,384},{1,129},{129,257},{257,385},{2,130},{1... | collective-permute-start | bytes 1572872 | tf_op jit(solution)/shard_map/ppermute | solution.py:14
  151.2 72.6 %collective-permute-start.5 = (bf16[64,4096]{1,0:T(8,128)(2,1)}, bf16[64,4096]{1,0:T(8,128)(2,1)S(1)}, u32[]{:S(2)}, u32[]{:S(2)}) collective-permute-start(bf16[64,4096]{1,0:T(8,128)(2,1)} %get-tuple-element.794), channel_id=1, source_target_pairs={{128,0},{256,128},{384,256},{129,1},{257,129},{385,257},{130,2},{2... | collective-permute-start | bytes 1572872 | tf_op jit(solution)/shard_map/ppermute | solution.py:14
  152.4 72.4 %collective-permute-start.4 = (bf16[64,4096]{1,0:T(8,128)(2,1)}, bf16[64,4096]{1,0:T(8,128)(2,1)}, u32[]{:S(2)}, u32[]{:S(2)}) collective-permute-start(bf16[64,4096]{1,0:T(8,128)(2,1)} %get-tuple-element.795), channel_id=1, source_target_pairs={{0,128},{128,256},{256,384},{1,129},{129,257},{257,385},{2,130},{1... | collective-permute-start | bytes 1572872 | tf_op jit(solution)/shard_map/ppermute | solution.py:14
  227.5 18.2 %all-to-all-start.6 = ((bf16[64,32,128]{2,0,1:T(8,128)(2,1)}), bf16[64,32,128]{2,0,1:T(8,128)(2,1)S(1)}, u32[]{:S(2)}, u32[]{:S(2)}) async-start(bf16[64,32,128]{2,0,1:T(8,128)(2,1)} %copy_bitcast_fusion.3), calls=%async_computation.6 | async-start | bytes 1048576 | tf_op jit(solution)/shard_map/cond/branch_1_fun/all_to_all | solution.py:145
  247.0 3.3 copy-start.18
  247.9 2.4 copy-start.118
  257.3 18.4 %all-to-all-start.7 = ((bf16[32,64,128]{2,1,0:T(8,128)(2,1)}), bf16[32,64,128]{2,1,0:T(8,128)(2,1)}, u32[]{:S(2)}, u32[]{:S(2)}) async-start(bf16[32,64,128]{2,1,0:T(8,128)(2,1)} %bitcast.1212), calls=%async_computation.7 | async-start | bytes 1048576 | tf_op jit(solution)/shard_map/cond/branch_1_fun/all_to_all | solution.py:149
  263.1 3.2 copy-start.74
  263.1 4.1 copy-start.95
  263.1 4.0 copy-start.104
  263.1 4.0 copy-start.119
  263.1 4.0 copy-start.125
  263.1 4.1 copy-start.82
  279.2 18.9 %all-to-all-start.8 = ((bf16[64,32,128]{2,0,1:T(8,128)(2,1)}), bf16[64,32,128]{2,0,1:T(8,128)(2,1)}, u32[]{:S(2)}, u32[]{:S(2)}) async-start(bf16[64,32,128]{2,0,1:T(8,128)(2,1)} %copy_bitcast_fusion.4), calls=%async_computation.8 | async-start | bytes 1048576 | tf_op jit(solution)/shard_map/cond/branch_1_fun/all_to_all | solution.py:145
  302.3 3.2 copy-start.50
  318.1 3.7 copy-start.26
  327.0 2.7 copy-start.37
  330.8 18.7 %all-to-all-start.9 = ((bf16[32,64,128]{2,1,0:T(8,128)(2,1)}), bf16[32,64,128]{2,1,0:T(8,128)(2,1)}, u32[]{:S(2)}, u32[]{:S(2)}) async-start(bf16[32,64,128]{2,1,0:T(8,128)(2,1)} %bitcast.1221), calls=%async_computation.9 | async-start | bytes 1048576 | tf_op jit(solution)/shard_map/cond/branch_1_fun/all_to_all | solution.py:149
  336.7 2.8 copy-start.38
  339.5 10.0 %copy-start.87 = (f32[4096]{0:T(1024)S(1)}, f32[4096]{0:T(1024)}, u32[]{:S(2)}) copy-start(f32[4096]{0:T(1024)} %get-tuple-element.436) | copy-start | bytes 49156 | tf_op jit(solution)/shard_map/cond
  353.7 7.3 %copy-start.86 = (f32[4096]{0:T(1024)S(1)}, f32[4096]{0:T(1024)}, u32[]{:S(2)}) copy-start(f32[4096]{0:T(1024)} %get-tuple-element.801) | copy-start | bytes 49156
  353.7 7.3 %copy-start.97 = (f32[2,2048,1,1]{1,3,2,0:T(1,128)S(1)}, f32[2,2048,1,1]{1,3,2,0:T(1,128)}, u32[]{:S(2)}) copy-start(f32[2,2048,1,1]{1,3,2,0:T(1,128)} %get-tuple-element.591) | copy-start | bytes 49156
  353.8 7.3 %copy-start.106 = (f32[2,2048,1,1]{1,3,2,0:T(1,128)S(1)}, f32[2,2048,1,1]{1,3,2,0:T(1,128)}, u32[]{:S(2)}) copy-start(f32[2,2048,1,1]{1,3,2,0:T(1,128)} %get-tuple-element.586) | copy-start | bytes 49156
  353.8 7.3 %copy-start.129 = (f32[2,64,1]{1,2,0:T(1,128)S(1)}, f32[2,64,1]{1,2,0:T(1,128)}, u32[]{:S(2)}) copy-start(f32[2,64,1]{1,2,0:T(1,128)} %get-tuple-element.585) | copy-start | bytes 1540
  354.9 2.8 collective-permute-start.7
  356.3 3.8 collective-permute-start.6
  357.8 3.3 copy-start.68
  363.3 82.9 %collective-permute-start.9 = (bf16[64,4096]{1,0:T(8,128)(2,1)S(1)}, bf16[64,4096]{1,0:T(8,128)(2,1)S(1)}, u32[]{:S(2)}, u32[]{:S(2)}) collective-permute-start(bf16[64,4096]{1,0:T(8,128)(2,1)S(1)} %get-tuple-element.788), channel_id=1, source_target_pairs={{0,128},{128,256},{256,384},{1,129},{129,257},{257,385},{2,130},{1... | collective-permute-start | bytes 1572872 | tf_op jit(solution)/shard_map/ppermute | solution.py:14
  444.7 5.5 collective-permute-start.8
  446.2 5.0 copy-start.67
  456.6 88.1 %copy-start.98 = (f32[2,2048,1,1]{1,3,2,0:T(1,128)S(1)}, f32[2,2048,1,1]{1,3,2,0:T(1,128)}, u32[]{:S(2)}) copy-start(f32[2,2048,1,1]{1,3,2,0:T(1,128)} %get-tuple-element.591) | copy-start | bytes 49156
  456.6 88.1 %copy-start.107 = (f32[2,2048,1,1]{1,3,2,0:T(1,128)S(1)}, f32[2,2048,1,1]{1,3,2,0:T(1,128)}, u32[]{:S(2)}) copy-start(f32[2,2048,1,1]{1,3,2,0:T(1,128)} %get-tuple-element.586) | copy-start | bytes 49156
  458.0 82.5 %collective-permute-start.11 = (bf16[64,4096]{1,0:T(8,128)(2,1)S(1)}, bf16[64,4096]{1,0:T(8,128)(2,1)S(1)}, u32[]{:S(2)}, u32[]{:S(2)}) collective-permute-start(bf16[64,4096]{1,0:T(8,128)(2,1)S(1)} %get-tuple-element.786), channel_id=1, source_target_pairs={{0,128},{128,256},{256,384},{1,129},{129,257},{257,385},{2,130},{1... | collective-permute-start | bytes 1572872 | tf_op jit(solution)/shard_map/ppermute | solution.py:14
  539.0 5.7 collective-permute-start.10
  546.7 18.2 %all-to-all-start.14 = ((bf16[64,32,128]{2,0,1:T(8,128)(2,1)}), bf16[64,32,128]{2,0,1:T(8,128)(2,1)S(1)}, u32[]{:S(2)}, u32[]{:S(2)}) async-start(bf16[64,32,128]{2,0,1:T(8,128)(2,1)} %copy_bitcast_fusion.7), calls=%async_computation.14 | async-start | bytes 1048576 | tf_op jit(solution)/shard_map/cond/branch_1_fun/all_to_all | solution.py:145
  552.3 4.2 copy-start.109
  552.3 4.2 copy-start.112
  569.4 5.0 copy-start.84
  574.3 2.9 copy-start.30
  579.6 4.9 copy-start.113
  583.0 4.2 copy-start.60
  583.0 4.2 copy-start.110
  583.0 4.2 copy-start.127
  645.4 3.4 collective-permute-start.12
  648.8 13.9 %collective-permute-start.13 = (bf16[1,4,128,128]{3,2,1,0:T(8,128)(2,1)S(1)}, bf16[1,4,128,128]{3,2,1,0:T(8,128)(2,1)S(1)}, u32[]{:S(2)}, u32[]{:S(2)}) collective-permute-start(bf16[1,4,128,128]{3,2,1,0:T(8,128)(2,1)S(1)} %collective-permute-done.12), channel_id=1, source_target_pairs={{0,256},{256,0},{128,384},{384,128},{1,257},{257,1},{129,385},{385... | collective-permute-start | bytes 393224 | tf_op jit(solution)/shard_map/ppermute | solution.py:24
  (34 other events, 56.3 us)
Sparse Core Ops, SparseCore 0:
  591.8 53.5 all-reduce.20
where the time goes:
time: 682 us; the launch traced here: 671 us
  starting transfers between devices  352 us (52%)
  waiting for transfers between devices  127 us (19%)
  other arithmetic  60.9 us (9%)
  matrix products  55.6 us (8%)
  local copies, waits for them, and re-layouts  47 us (7%)
  loops' own time  15 us (2%)
  between operations  13.9 us (2%)
    ppermute x12, starting transfers between devices, from_behind(): lax.ppermute(value, axis, [(source, source + steps) for source in range(f...  299 us
    psum x1, waiting for transfers between devices, local(): lax.psum(mirror_grads.astype(jnp.bfloat16), 'dp').astype(jnp.float32)  53.7 us
    dot_general x31, matrix products, mix(): return jnp.einsum(form, left, right, preferred_element_type=jnp.float32)  49.1 us
    all_to_all x4, waiting for transfers between devices, head_layout(): lax.all_to_all(values, 'seq', split_axis=1, concat_axis=0, tiled=True)  37.2 us
    all_to_all x4, starting transfers between devices, head_layout(): lax.all_to_all(values, 'seq', split_axis=1, concat_axis=0, tiled=True)  27.7 us
    all_to_all x3, starting transfers between devices, token_layout(): lax.all_to_all(values, 'seq', split_axis=0, concat_axis=1, tiled=True)  17.2 us
  transfers between devices with their start and end apart: 22, of which 17 were waited for; matrix products, arithmetic and copies ran while one was open for 6% of the time, Pallas kernels for 0%

commit v1 on v0

v1 whole, which is shorter than its diff:
```python
import functools

import jax
import jax.numpy as jnp
from jax import lax
from jax.experimental import pallas as pl
from jax.experimental.pallas import tpu as pltpu
from jax.sharding import PartitionSpec as P

EPSILON = 1e-06
SECTIONS = 4
SPAN = 64
HEAD = 128
GROUP = 128
F32 = jnp.float32
BF16 = jnp.bfloat16
LOG2E = 1.4426950408889634


def dot(a, b):
    return lax.dot_general(a, b, (((1,), (0,)), ((), ())), preferred_element_type=F32)


def dot_nt(a, b):
    return lax.dot_general(a, b, (((1,), (1,)), ((), ())), preferred_element_type=F32)


def dot_tn(a, b):
    return lax.dot_general(a, b, (((0,), (0,)), ((), ())), preferred_element_type=F32)


def kernel(
    cfg,
    inputs_ref,
    weights_ref,
    gains_ref,
    docs_ref,
    grads_ref,
    states,
    normed,
    queries,
    keys,
    values,
    mixed,
    chances,
    scale_q,
    scale_k,
    scale_x,
    mask,
    valid,
    cot,
    grad_mixed,
    grad_normed,
    grad_q,
    grad_k,
    grad_v,
    carry,
    sums,
    gain_rows,
    send1,
    recv1,
    send2,
    recv2,
    in_send,
    in_recv,
    send1_sem,
    recv1_sem,
    send2_sem,
    recv2_sem,
):
    total, seq, width, across = cfg["total"], cfg["seq"], cfg["width"], cfg["across"]
    rows, chunk, chunks = cfg["rows"], cfg["chunk"], cfg["chunks"]
    down = seq // across
    groups, blocks = chunk // GROUP, chunk // SPAN
    all_blocks = rows // SPAN
    place, me = lax.axis_index("pipe"), lax.axis_index("seq")
    micro, half = place // 2, place % 2
    first_block = half * (seq - all_blocks)
    window = first_block * SPAN
    my_x, my_y = me % across, me // across

    barrier = pltpu.get_barrier_semaphore()

    def greet(o, _):
        pl.semaphore_signal(barrier, inc=1, device_id={"seq": (me + o) % seq})
        return 0

    lax.fori_loop(1, seq, greet, 0)
    pl.semaphore_wait(barrier, seq - 1)

    slot = me - first_block
    in_window = (slot >= 0) & (slot < all_blocks)

    def piece(head):
        return inputs_ref.at[0, micro, :, pl.ds(pl.multiple_of(head * HEAD, HEAD), HEAD)]

    @pl.when(in_window)
    def _():
        landing = states.at[0, pl.ds(pl.multiple_of(slot * SPAN, SPAN), SPAN)]

        def send(o, _):
            peer = (me + o) % seq
            pltpu.make_async_remote_copy(
                src_ref=piece(peer),
                dst_ref=landing,
                send_sem=in_send,
                recv_sem=in_recv,
                device_id={"seq": peer},
            ).start()
            return 0

        lax.fori_loop(1, seq, send, 0)
        pltpu.make_async_copy(piece(me), landing, in_recv).start()

    ones = jnp.full((HEAD, HEAD), 1.0 / HEAD, BF16)
    row8 = lax.broadcasted_iota(jnp.int32, (8, HEAD), 0)

    both = docs_ref[0].astype(F32)
    lengths = jnp.where(micro == 0, both[0:1], both[1:2]).astype(BF16)
    count = lengths.shape[1]
    earlier = lax.broadcasted_iota(jnp.int32, (count, HEAD), 0) < lax.broadcasted_iota(
        jnp.int32, (count, HEAD), 1
    )
    starts = dot(jnp.broadcast_to(lengths, (8, count)), jnp.where(earlier, 1.0, 0.0).astype(BF16))[:1]
    mid = total // 2

    def make_mask(b, _):
        base = window + b * SPAN
        token = base + lax.broadcasted_iota(jnp.int32, (SPAN, HEAD), 0)
        key = base - SPAN + lax.broadcasted_iota(jnp.int32, (SPAN, HEAD), 1)
        reach = jnp.where(starts <= token.astype(F32), starts, 0.0)
        begin = jnp.max(reach, axis=1, keepdims=True)
        allowed = (key.astype(F32) >= begin) & (key <= token)
        mask[b] = jnp.where(allowed, 1.0, 0.0)
        late = jnp.where(begin >= mid, 1.0, 0.0)
        mine = jnp.where(half == 1, late, 1.0 - late)
        valid[pl.ds(pl.multiple_of(b * SPAN, SPAN), SPAN)] = jnp.broadcast_to(mine, (SPAN, HEAD)).astype(BF16)
        return 0

    lax.fori_loop(0, all_blocks, make_mask, 0)
    for s in range(SECTIONS):
        keys[s, :SPAN] = jnp.zeros((SPAN, HEAD), BF16)
        values[s, :SPAN] = jnp.zeros((SPAN, HEAD), BF16)
        gain = gains_ref[s : s + 1, pl.ds(pl.multiple_of(me * HEAD, HEAD), HEAD)]
        gain_rows[s] = jnp.broadcast_to(gain, (8, HEAD))
    sums[...] = jnp.zeros_like(sums)

    def packed(terms):
        total_rows = None
        for g, term in enumerate(terms):
            pick = jnp.where(row8 == g, 1.0, 0.0).astype(BF16)
            part = dot_nt(pick, term.astype(BF16))
            total_rows = part if total_rows is None else total_rows + part
        return total_rows

    def spread(row):
        return jnp.transpose(jnp.broadcast_to(row, (HEAD, GROUP)))

    def start1(item, part):
        send1[item] = part
        for o in range(1, across):
            pltpu.make_async_remote_copy(
                src_ref=send1.at[item],
                dst_ref=recv1.at[item, o - 1],
                send_sem=send1_sem.at[item],
                recv_sem=recv1_sem.at[item],
                device_id={"seq": my_y * across + (my_x + o) % across},
            ).start()

    def start2(item):
        pltpu.make_async_copy(recv1.at[item], recv1.at[item], recv1_sem.at[item]).wait()
        part = send1[item]
        for o in range(across - 1):
            part = part + recv1[item, o]
        send2[item] = part
        for o in range(1, down):
            pltpu.make_async_remote_copy(
                src_ref=send2.at[item],
                dst_ref=recv2.at[item, o - 1],
                send_sem=send2_sem.at[item],
                recv_sem=recv2_sem.at[item],
                device_id={"seq": ((my_y + o) % down) * across + my_x},
            ).start()

    def finish(item):
        pltpu.make_async_copy(recv2.at[item], recv2.at[item], recv2_sem.at[item]).wait()
        part = send2[item]
        for o in range(down - 1):
            part = part + recv2[item, o]
        return part

    def span_of(start, size):
        return pl.ds(pl.multiple_of(start, SPAN), size)

    def gain_of(s):
        return gain_rows[s][:1]

    pltpu.make_async_copy(states.at[0], states.at[0], in_recv).wait()

    def begin(c, _):
        terms = []
        for g in range(groups):
            x = states[0, span_of(c * chunk + g * GROUP, GROUP)].astype(F32)
            terms.append(x * x)
        start1(c, packed(terms))
        return 0

    lax.fori_loop(0, chunks, begin, 0)
    lax.fori_loop(0, chunks, lambda c, _: (start2(c), 0)[1], 0)

    def forward(i, _):
        s, c = i // chunks, i % chunks
        base = c * chunk
        rs = lax.rsqrt(finish(i) * (1.0 / width) + EPSILON)
        gain = gain_of(s)
        for g in range(groups):
            at = span_of(base + g * GROUP, GROUP)
            padded = span_of(base + g * GROUP + SPAN, GROUP)
            wide = spread(rs[g : g + 1])
            scale_x[s, at] = wide
            xn = (states[s, at].astype(F32) * wide * gain).astype(BF16)
            normed[s, at] = xn
            q = dot(xn, weights_ref[s, 0, 0])
            k = dot(xn, weights_ref[s, 0, 1])
            values[s, padded] = dot(xn, weights_ref[s, 0, 2]).astype(BF16)
            rq = lax.rsqrt(dot((q * q).astype(BF16), ones) + EPSILON)
            rk = lax.rsqrt(dot((k * k).astype(BF16), ones) + EPSILON)
            scale_q[s, at] = rq
            scale_k[s, at] = rk
            queries[s, at] = (q * rq).astype(BF16)
            keys[s, padded] = (k * rk).astype(BF16)
        for b in range(blocks):
            at = span_of(base + b * SPAN, SPAN)
            near = span_of(base + b * SPAN, 2 * SPAN)
            scores = dot_nt(queries[s, at], keys[s, near])
            raised = jnp.exp2(scores * (LOG2E * HEAD**-0.5)) * mask[c * blocks + b]
            share = (raised / jnp.sum(raised, axis=1, keepdims=True)).astype(BF16)
            chances[s, c * blocks + b] = share
            mixed[s, at] = dot(share, values[s, near]).astype(BF16)
        terms = []
        for g in range(groups):
            at = span_of(base + g * GROUP, GROUP)
            branch = dot(mixed[s, at], weights_ref[s, 0, 3]).astype(BF16)
            new = (states[s, at].astype(F32) + branch.astype(F32)).astype(BF16)
            states[s + 1, at] = new
            new = new.astype(F32)
            terms.append(new * new)

        @pl.when(s < SECTIONS - 1)
        def _():
            start1(i + chunks, packed(terms))

        @pl.when((i >= 1) & (i <= (SECTIONS - 1) * chunks))
        def _():
            start2(i + chunks - 1)

        return 0

    lax.fori_loop(0, SECTIONS * chunks, forward, 0)

    offset = SECTIONS * chunks

    def backward(j, _):
        s, c = SECTIONS - 1 - j // chunks, chunks - 1 - j % chunks
        base = c * chunk

        @pl.when(j < chunks)
        def _():
            at = span_of(base, chunk)
            cot[at] = states[SECTIONS, at] * valid[at]

        @pl.when(j >= chunks)
        def _():
            along = finish(offset + j - chunks) * (1.0 / width)
            gain = gain_of(s + 1)
            for g in range(groups):
                at = span_of(base + g * GROUP, GROUP)
                wide = scale_x[s + 1, at]
                pulled = grad_normed[at].astype(F32) * gain
                unit = states[s + 1, at].astype(F32) * wide
                fresh = cot[at].astype(F32) + wide * (pulled - unit * spread(along[g : g + 1]))
                cot[at] = fresh.astype(BF16)

        @pl.when(c == chunks - 1)
        def _():
            carry[...] = jnp.zeros_like(carry)

        for g in range(groups):
            at = span_of(base + g * GROUP, GROUP)
            grad_mixed[pl.ds(g * GROUP, GROUP)] = dot_nt(cot[at], weights_ref[s, 0, 3]).astype(BF16)
        whole = span_of(base, chunk)
        sums[s, 3] += dot_tn(mixed[s, whole], cot[whole])

        late_k, late_v = carry[0], carry[1]
        for b in reversed(range(blocks)):
            at = span_of(base + b * SPAN, SPAN)
            near = span_of(base + b * SPAN, 2 * SPAN)
            here = pl.ds(b * SPAN, SPAN)
            gm = grad_mixed[here]
            share = chances[s, c * blocks + b]
            wide_share = share.astype(F32)
            grad_share = dot_nt(gm, values[s, near])
            mean = jnp.sum(grad_share * wide_share, axis=1, keepdims=True)
            grad_score = (wide_share * (grad_share - mean) * (HEAD**-0.5)).astype(BF16)
            qn = queries[s, at]
            unit_v = dot_tn(share, gm)
            unit_k = dot_tn(grad_score, qn)
            unit_q = dot(grad_score, keys[s, near])
            along = dot((unit_q * qn.astype(F32)).astype(BF16), ones)
            grad_q[here] = (scale_q[s, at] * (unit_q - qn.astype(F32) * along)).astype(BF16)
            grad_v[here] = (unit_v[SPAN:] + late_v).astype(BF16)
            mine_k = unit_k[SPAN:] + late_k
            kn = keys[s, span_of(base + b * SPAN + SPAN, SPAN)].astype(F32)
            along = dot((mine_k * kn).astype(BF16), ones)
            grad_k[here] = (scale_k[s, at] * (mine_k - kn * along)).astype(BF16)
            late_k, late_v = unit_k[:SPAN], unit_v[:SPAN]
        carry[0] = late_k
        carry[1] = late_v

        xn = normed[s, whole]
        sums[s, 0] += dot_tn(xn, grad_q[...])
        sums[s, 1] += dot_tn(xn, grad_k[...])
        sums[s, 2] += dot_tn(xn, grad_v[...])

        @pl.when(s > 0)
        def _():
            terms = []
            for g in range(groups):
                at = span_of(base + g * GROUP, GROUP)
                here = pl.ds(g * GROUP, GROUP)
                grad = dot_nt(grad_q[here], weights_ref[s, 0, 0])
                grad = grad + dot_nt(grad_k[here], weights_ref[s, 0, 1])
                grad = grad + dot_nt(grad_v[here], weights_ref[s, 0, 2])
                grad = grad.astype(BF16)
                grad_normed[at] = grad
                terms.append(grad.astype(F32) * normed[s, at].astype(F32))
            start1(offset + j, packed(terms))

        @pl.when((j >= 1) & (j <= (SECTIONS - 1) * chunks))
        def _():
            start2(offset + j - 1)

        return 0

    lax.fori_loop(0, SECTIONS * chunks, backward, 0)

    grads_ref[...] = sums[...].astype(BF16)

    def drain(item, _):
        pltpu.make_async_copy(recv1.at[item], recv1.at[item], send1_sem.at[item]).wait()
        pltpu.make_async_copy(recv2.at[item], recv2.at[item], send2_sem.at[item]).wait()
        return 0

    lax.fori_loop(0, offset + (SECTIONS - 1) * chunks, drain, 0)

    @pl.when(in_window)
    def _():
        def settle(o, _):
            pltpu.make_async_copy(piece(me), piece(me), in_send).wait()
            return 0

        lax.fori_loop(1, seq, settle, 0)


def local(inputs, weights, gains, doc_lengths):
    seq = lax.axis_size("seq")
    total = inputs.shape[2] * seq
    width = gains.shape[1]
    rows = total // 2 + 2 * SPAN
    chunks = 3 if rows % (3 * GROUP) == 0 else 2
    chunk = rows // chunks
    across = 4 if seq > 4 else 2
    down = seq // across
    items = (2 * SECTIONS - 1) * chunks
    cfg = dict(total=total, seq=seq, width=width, across=across, rows=rows, chunk=chunk, chunks=chunks)
    scratch = [
        pltpu.VMEM((SECTIONS + 1, rows, HEAD), BF16),
        pltpu.VMEM((SECTIONS, rows, HEAD), BF16),
        pltpu.VMEM((SECTIONS, rows, HEAD), BF16),
        pltpu.VMEM((SECTIONS, SPAN + rows, HEAD), BF16),
        pltpu.VMEM((SECTIONS, SPAN + rows, HEAD), BF16),
        pltpu.VMEM((SECTIONS, rows, HEAD), BF16),
        pltpu.VMEM((SECTIONS, rows // SPAN, SPAN, 2 * SPAN), BF16),
        pltpu.VMEM((SECTIONS, rows, HEAD), F32),
        pltpu.VMEM((SECTIONS, rows, HEAD), F32),
        pltpu.VMEM((SECTIONS, rows, HEAD), F32),
        pltpu.VMEM((rows // SPAN, SPAN, 2 * SPAN), F32),
        pltpu.VMEM((rows, HEAD), BF16),
        pltpu.VMEM((rows, HEAD), BF16),
        pltpu.VMEM((chunk, HEAD), BF16),
        pltpu.VMEM((rows, HEAD), BF16),
        pltpu.VMEM((chunk, HEAD), BF16),
        pltpu.VMEM((chunk, HEAD), BF16),
        pltpu.VMEM((chunk, HEAD), BF16),
        pltpu.VMEM((2, SPAN, HEAD), F32),
        pltpu.VMEM((SECTIONS, 4, HEAD, HEAD), F32),
        pltpu.VMEM((SECTIONS, 8, HEAD), F32),
        pltpu.VMEM((items, 8, HEAD), F32),
        pltpu.VMEM((items, across - 1, 8, HEAD), F32),
        pltpu.VMEM((items, 8, HEAD), F32),
        pltpu.VMEM((items, down - 1, 8, HEAD), F32),
        pltpu.SemaphoreType.DMA,
        pltpu.SemaphoreType.DMA,
        pltpu.SemaphoreType.DMA((items,)),
        pltpu.SemaphoreType.DMA((items,)),
        pltpu.SemaphoreType.DMA((items,)),
        pltpu.SemaphoreType.DMA((items,)),
    ]
    vmem = pl.BlockSpec(memory_space=pltpu.VMEM)
    grads = pl.pallas_call(
        functools.partial(kernel, cfg),
        out_shape=jax.ShapeDtypeStruct((SECTIONS, 4, HEAD, HEAD), BF16),
        in_specs=[pl.BlockSpec(memory_space=pl.ANY), vmem, vmem, vmem],
        out_specs=vmem,
        scratch_shapes=scratch,
        compiler_params=pltpu.CompilerParams(
            collective_id=0, has_side_effects=True, vmem_limit_bytes=50 * 1024 * 1024
        ),
    )(inputs, weights, gains, doc_lengths)
    own = lax.psum_scatter(grads, "pipe", scatter_dimension=0, tiled=True)
    return lax.psum(own, "dp").astype(F32)[:, None]


def solution(mesh):
    placed = (
        P("dp", None, "seq", None),
        P(None, "seq", None, None, None),
        P(),
        P("dp", None, None),
    )
    return jax.shard_map(
        local,
        mesh=mesh,
        in_specs=placed,
        out_specs=P("pipe", "seq", None, None, None),
        check_vma=False,
    )
```

time: 682 us -> 239 us (0.35); the launches traced: 671 us -> 239 us
  starting transfers between devices: 352 us -> 0.04 us
  Pallas kernels: 0 us -> 120 us
  other arithmetic: 60.9 us -> 1.62 us
  matrix products: 55.6 us -> 0 us
  local copies, waits for them, and re-layouts: 47 us -> 3.78 us
  waiting for transfers between devices: 127 us -> 99.9 us
  loops' own time: 15 us -> 0 us
    ppermute x14 -> x0, starting transfers between devices: 307 us -> none  [the longest x12 299 us: from_behind(): lax.ppermute(value, axis, [(source, source + steps) for source in range(f...]
    pallas_call x0 -> x1, Pallas kernels: none -> 120 us  [local(): pl.pallas_call(functools.partial(kernel, cfg), out_shape=jax.ShapeDtypeSt...]
    all_to_all x7 -> x0, waiting for transfers between devices: 50.4 us -> none  [the longest x4 37.2 us: head_layout(): lax.all_to_all(values, 'seq', split_axis=1, concat_axis=0, tiled=True)]
    dot_general x31 -> x0, matrix products: 49.1 us -> none  [mix(): return jnp.einsum(form, left, right, preferred_element_type=jnp.float32)]
    reduce_scatter x0 -> x1, waiting for transfers between devices: none -> 45.8 us  [local(): own = lax.psum_scatter(grads, 'pipe', scatter_dimension=0, tiled=True)]
    all_to_all x7 -> x0, starting transfers between devices: 44.9 us -> none  [the longest x4 27.7 us: head_layout(): lax.all_to_all(values, 'seq', split_axis=1, concat_axis=0, tiled=True)]
    ppermute x14 -> x0, waiting for transfers between devices: 23.3 us -> none  [the longest x12 13.2 us: from_behind(): lax.ppermute(value, axis, [(source, source + steps) for source in range(f...]
    select_n x16 -> x0, other arithmetic: 17.5 us -> none  [the longest x3 6.88 us: local(): up_x = jnp.where(use_up, stepped, up_x)]
  transfers between devices with their start and end apart: 22 -> 2, of which waited for: 17 -> 2; matrix products, arithmetic and copies ran while one was open for 6% -> 0% of each run, Pallas kernels for 0% -> 0%
where the time goes in v1:
time: 239 us
  Pallas kernels  120 us (50%)
  waiting for transfers between devices  99.9 us (42%)
  between operations  13.4 us (6%)
  local copies, waits for them, and re-layouts  3.78 us (2%)
    pallas_call x1, Pallas kernels, local(): pl.pallas_call(functools.partial(kernel, cfg), out_shape=jax.ShapeDtypeSt...  120 us
    psum x1, waiting for transfers between devices, local(): return lax.psum(own, 'dp').astype(F32)[:, None]  54.1 us
    reduce_scatter x1, waiting for transfers between devices, local(): own = lax.psum_scatter(grads, 'pipe', scatter_dimension=0, tiled=True)  45.8 us
  transfers between devices with their start and end apart: 2, of which 2 were waited for; matrix products, arithmetic and copies ran while one was open for 0% of the time, Pallas kernels for 0%

profile of v1, /device:TPU:6, one launch (start us, length us, event | category | flops | bytes accessed | tf_op | source)
XLA Modules:
  0.0 239.0 jit_solution(13925516317081542720)
XLA Ops:
  6.5 0.0 reduce-scatter.2.cloned.1.call-start
  6.5 0.0 copy-start
  6.5 1.2 copy-done
  7.8 0.0 copy-start.1
  7.8 1.0 copy-done.1
  8.8 0.0 copy-start.2
  8.8 0.8 copy-done.2
  9.6 0.0 copy-start.3
  9.6 0.7 copy-done.3
  10.3 120.2 %shard_map.46 = bf16[4,4,128,128]{3,2,1,0:T(8,128)(2,1)} custom-call(bf16[1,2,64,4096]{3,2,1,0:T(8,128)(2,1)S(1)} %copy-done, bf16[4,1,4,128,128]{4,3,2,1,0:T(8,128)(2,1)S(1)} %copy-done.1, f32[4,4096]{1,0:T(4,128)S(1)} %copy-done.2, s32[1,2,48]{2,1,0:T(2,128)S(1)} %copy-done.3), custom_call_target="tpu_custom_call" | custom-call | tf_op jit(solution)/shard_map/pallas_call | solution.py:410
  130.5 0.0 reduce-scatter.2.cloned.1.call-update
  130.6 0.0 all-reduce.2.cloned.1.call-start
  130.6 45.8 %reduce-scatter.2.cloned.1.call-done = bf16[1,4,128,128]{3,2,1,0:T(8,128)(2,1)} async-done(((bf16[4,4,128,128]{3,2,1,0:T(8,128)(2,1)}), bf16[1,4,128,128]{3,2,1,0:T(8,128)(2,1)}) %reduce-scatter.2.cloned.1.call-update) | async-done | bytes 131088 | tf_op jit(solution)/shard_map/reduce_scatter | solution.py:420
  176.4 0.0 all-reduce.2.cloned.1.call-update
  176.4 54.1 %all-reduce.2.cloned.1.call-done = bf16[1,1,4,128,128]{4,3,2,1,0:T(8,128)(2,1)} async-done(((bf16[1,1,4,128,128]{4,3,2,1,0:T(8,128)(2,1)}), bf16[1,1,4,128,128]{4,3,2,1,0:T(8,128)(2,1)}) %all-reduce.2.cloned.1.call-update) | async-done | bytes 131088 | tf_op jit(solution)/shard_map/psum | solution.py:421
  230.5 1.6 broadcast_in_dim.7
Async XLA Ops:
  6.5 169.8 %reduce-scatter.2.cloned.1.call-start = ((), (), s32[]{:S(2)}) async-start(), calls=%async_computation.1 | async-start | bytes 655360 | tf_op jit(solution)/shard_map/reduce_scatter | solution.py:420
  6.5 1.2 copy-start
  7.8 1.0 copy-start.1
  8.8 0.8 copy-start.2
  9.6 0.7 copy-start.3
  130.6 100.0 %all-reduce.2.cloned.1.call-start = ((), (), s32[]{:S(2)}) async-start(), calls=%async_computation.2 | async-start | bytes 262144 | tf_op jit(solution)/shard_map/psum | solution.py:421
Sparse Core Ops, SparseCore 0:
  130.7 45.6 reduce-scatter.1
  179.5 50.9 all-reduce.1

commit v2 on v1

v2 whole, which is shorter than its diff:
```python
import functools

import jax
import jax.numpy as jnp
from jax import lax
from jax.experimental import pallas as pl
from jax.experimental.pallas import tpu as pltpu
from jax.sharding import PartitionSpec as P

EPSILON = 1e-06
SECTIONS = 4
SPAN = 64
HEAD = 128
GROUP = 128
F32 = jnp.float32
BF16 = jnp.bfloat16
LOG2E = 1.4426950408889634


def dot(a, b):
    return lax.dot_general(a, b, (((1,), (0,)), ((), ())), preferred_element_type=F32)


def dot_nt(a, b):
    return lax.dot_general(a, b, (((1,), (1,)), ((), ())), preferred_element_type=F32)


def dot_tn(a, b):
    return lax.dot_general(a, b, (((0,), (0,)), ((), ())), preferred_element_type=F32)


def kernel(
    cfg,
    inputs_ref,
    weights_ref,
    gains_ref,
    docs_ref,
    grads_ref,
    weights,
    gains,
    docs,
    weights_in,
    weights_back,
    states,
    normed,
    queries,
    keys,
    values,
    mixed,
    chances,
    scale_q,
    scale_k,
    scale_x,
    mask,
    valid,
    cot,
    grad_normed,
    carry,
    sums,
    gain_rows,
    send1,
    recv1,
    send2,
    recv2,
    half_send,
    half_recv,
    chip_send,
    chip_recv,
    own_send,
    own_recv,
    load_sem,
    in_send,
    in_recv,
    send1_sem,
    recv1_sem,
    send2_sem,
    recv2_sem,
    half_send_sem,
    half_recv_sem,
    chip_send_sem,
    chip_recv_sem,
    own_send_sem,
    own_recv_sem,
):
    total, seq, width, across = cfg["total"], cfg["seq"], cfg["width"], cfg["across"]
    rows, chunk, chunks = cfg["rows"], cfg["chunk"], cfg["chunks"]
    pipe, dp = cfg["pipe"], cfg["dp"]
    down = seq // across
    groups, blocks = chunk // GROUP, chunk // SPAN
    all_blocks = rows // SPAN
    place, me, replica = lax.axis_index("pipe"), lax.axis_index("seq"), lax.axis_index("dp")
    micro, half = place // 2, place % 2
    core = half
    chip = micro * dp + replica
    first_block = half * (seq - all_blocks)
    window = first_block * SPAN
    my_x, my_y = me % across, me // across

    loads = [
        pltpu.make_async_copy(weights_ref.at[:, 0], weights, load_sem.at[0]),
        pltpu.make_async_copy(
            gains_ref.at[:, pl.ds(pl.multiple_of(me * HEAD, HEAD), HEAD)], gains, load_sem.at[1]
        ),
        pltpu.make_async_copy(docs_ref.at[0], docs, load_sem.at[2]),
    ]
    for load in loads:
        load.start()

    barrier = pltpu.get_barrier_semaphore()

    def greet(o, _):
        pl.semaphore_signal(barrier, inc=1, device_id={"seq": (me + o) % seq})
        return 0

    def greet_column(o, _):
        other = (place * dp + replica + o) % (pipe * dp)
        pl.semaphore_signal(barrier, inc=1, device_id={"pipe": other // dp, "dp": other % dp})
        return 0

    lax.fori_loop(1, seq, greet, 0)
    lax.fori_loop(1, pipe * dp, greet_column, 0)
    pl.semaphore_wait(barrier, seq - 1 + pipe * dp - 1)

    slot = me - first_block
    in_window = (slot >= 0) & (slot < all_blocks)

    def piece(head):
        return inputs_ref.at[0, micro, :, pl.ds(pl.multiple_of(head * HEAD, HEAD), HEAD)]

    @pl.when(in_window)
    def _():
        landing = states.at[0, pl.ds(pl.multiple_of(slot * SPAN, SPAN), SPAN)]

        def send(o, _):
            peer = (me + o) % seq
            pltpu.make_async_remote_copy(
                src_ref=piece(peer),
                dst_ref=landing,
                send_sem=in_send,
                recv_sem=in_recv,
                device_id={"seq": peer},
            ).start()
            return 0

        lax.fori_loop(1, seq, send, 0)
        pltpu.make_async_copy(piece(me), landing, in_recv).start()

    ones = jnp.full((HEAD, HEAD), 1.0, BF16)
    mean = jnp.full((HEAD, HEAD), 1.0 / HEAD, BF16)
    row8 = lax.broadcasted_iota(jnp.int32, (8, HEAD), 0)
    row16 = lax.broadcasted_iota(jnp.int32, (16, groups * HEAD), 0) % 8
    lane16 = lax.broadcasted_iota(jnp.int32, (16, groups * HEAD), 1) // HEAD
    selector = jnp.where(row16 == lane16, 1.0, 0.0).astype(BF16)

    for load in loads:
        load.wait()

    both = docs[...].astype(F32)
    lengths = jnp.where(micro == 0, both[0:1], both[1:2]).astype(BF16)
    count = lengths.shape[1]
    earlier = lax.broadcasted_iota(jnp.int32, (count, HEAD), 0) < lax.broadcasted_iota(
        jnp.int32, (count, HEAD), 1
    )
    starts = dot(jnp.broadcast_to(lengths, (8, count)), jnp.where(earlier, 1.0, 0.0).astype(BF16))[:1]
    mid = total // 2

    def make_mask(b, _):
        base = window + b * SPAN
        token = base + lax.broadcasted_iota(jnp.int32, (SPAN, HEAD), 0)
        key = base - SPAN + lax.broadcasted_iota(jnp.int32, (SPAN, HEAD), 1)
        reach = jnp.where(starts <= token.astype(F32), starts, 0.0)
        begin = jnp.max(reach, axis=1, keepdims=True)
        allowed = (key.astype(F32) >= begin) & (key <= token)
        mask[b] = jnp.where(allowed, 1.0, 0.0)
        late = jnp.where(begin >= mid, 1.0, 0.0)
        mine = jnp.where(half == 1, late, 1.0 - late)
        valid[pl.ds(pl.multiple_of(b * SPAN, SPAN), SPAN)] = jnp.broadcast_to(mine, (SPAN, HEAD)).astype(BF16)
        return 0

    lax.fori_loop(0, all_blocks, make_mask, 0)
    for s in range(SECTIONS):
        keys[s, :SPAN] = jnp.zeros((SPAN, HEAD), BF16)
        values[s, :SPAN] = jnp.zeros((SPAN, HEAD), BF16)
        gain_rows[s] = jnp.broadcast_to(gains[s : s + 1], (8, HEAD))
    sums[...] = jnp.zeros_like(sums)

    def arrange(s, _):
        for m in range(4):
            block = weights[s, m]
            if m < 3:
                weights_in[s, :, m * HEAD : (m + 1) * HEAD] = block
            weights_back[s, m * HEAD : (m + 1) * HEAD] = jnp.transpose(block.astype(F32)).astype(BF16)
        return 0

    lax.fori_loop(0, SECTIONS, arrange, 0)

    def packed(term):
        total_rows = None
        for g in range(groups):
            pick = jnp.where(row8 == g, 1.0, 0.0).astype(BF16)
            part = dot_nt(pick, term[g * GROUP : (g + 1) * GROUP])
            total_rows = part if total_rows is None else total_rows + part
        return total_rows

    def spread(packed_rows):
        high = packed_rows.astype(BF16)
        low = (packed_rows - high.astype(F32)).astype(BF16)
        wide = dot_tn(jnp.concatenate([high, low], axis=0), selector)
        return jnp.concatenate([wide[:, g * HEAD : (g + 1) * HEAD] for g in range(groups)], axis=0)

    def start1(item, part):
        send1[item] = part
        for o in range(1, across):
            pltpu.make_async_remote_copy(
                src_ref=send1.at[item],
                dst_ref=recv1.at[item, o - 1],
                send_sem=send1_sem.at[item],
                recv_sem=recv1_sem.at[item],
                device_id={"seq": my_y * across + (my_x + o) % across},
            ).start()

    def start2(item):
        pltpu.make_async_copy(recv1.at[item], recv1.at[item], recv1_sem.at[item]).wait()
        part = send1[item]
        for o in range(across - 1):
            part = part + recv1[item, o]
        send2[item] = part
        for o in range(1, down):
            pltpu.make_async_remote_copy(
                src_ref=send2.at[item],
                dst_ref=recv2.at[item, o - 1],
                send_sem=send2_sem.at[item],
                recv_sem=recv2_sem.at[item],
                device_id={"seq": ((my_y + o) % down) * across + my_x},
            ).start()

    def finish(item):
        pltpu.make_async_copy(recv2.at[item], recv2.at[item], recv2_sem.at[item]).wait()
        part = send2[item]
        for o in range(down - 1):
            part = part + recv2[item, o]
        return part

    def span_of(start, size):
        return pl.ds(pl.multiple_of(start, SPAN), size)

    def gain_of(s):
        return gain_rows[s][:1]

    def cut(value, b, size=SPAN):
        return value[b * SPAN : b * SPAN + size]

    def start_halves(s):
        for m in range(2):
            theirs = jnp.where(core == 0, sums[s, 2 + m], sums[s, m])
            half_send[s, m] = theirs.astype(BF16)
        pltpu.make_async_remote_copy(
            src_ref=half_send.at[s],
            dst_ref=half_recv.at[s],
            send_sem=half_send_sem.at[s],
            recv_sem=half_recv_sem.at[s],
            device_id={"pipe": micro * 2 + 1 - core},
        ).start()

    def start_chips(s):
        pltpu.make_async_copy(half_recv.at[s], half_recv.at[s], half_recv_sem.at[s]).wait()
        for m in range(2):
            ours = jnp.where(core == 0, sums[s, m], sums[s, 2 + m])
            chip_send[s, m] = (ours + half_recv[s, m].astype(F32)).astype(BF16)
        for m in range(2):
            owner = core * 2 + m
            here = (place == s) & (replica == owner)

            @pl.when(here)
            def _():
                pltpu.make_async_copy(chip_send.at[s, m], chip_recv.at[chip], chip_recv_sem).start()

            @pl.when(jnp.logical_not(here))
            def _():
                pltpu.make_async_remote_copy(
                    src_ref=chip_send.at[s, m],
                    dst_ref=chip_recv.at[chip],
                    send_sem=chip_send_sem.at[s],
                    recv_sem=chip_recv_sem,
                    device_id={"pipe": s, "dp": owner},
                ).start()

    def own_sum():
        pltpu.make_async_copy(chip_recv, chip_recv, chip_recv_sem).wait()
        part = chip_recv[0].astype(F32)
        for k in range(1, 2 * dp):
            part = part + chip_recv[k].astype(F32)
        own_send[...] = part.astype(BF16)
        for o in range(1, dp):
            pltpu.make_async_remote_copy(
                src_ref=own_send,
                dst_ref=own_recv.at[o - 1],
                send_sem=own_send_sem,
                recv_sem=own_recv_sem,
                device_id={"dp": (replica + o) % dp},
            ).start()
        grads_ref[0, 0, replica] = part
        pltpu.make_async_copy(own_recv, own_recv, own_recv_sem).wait()
        for o in range(1, dp):
            grads_ref[0, 0, (replica - o + dp) % dp] = own_recv[o - 1].astype(F32)

    pltpu.make_async_copy(states.at[0], states.at[0], in_recv).wait()

    def begin(c, _):
        x = states[0, span_of(c * chunk, chunk)].astype(F32)
        start1(c, packed((x * x).astype(BF16)))
        return 0

    lax.fori_loop(0, chunks, begin, 0)
    lax.fori_loop(0, chunks, lambda c, _: (start2(c), 0)[1], 0)

    def forward(i, _):
        s, c = i // chunks, i % chunks
        base = c * chunk
        whole = span_of(base, chunk)
        padded = span_of(base + SPAN, chunk)
        rs = lax.rsqrt(finish(i) * (1.0 / width) + EPSILON)
        wide = spread(rs)
        x = states[s, whole].astype(F32)
        xn = (x * wide * gain_of(s)).astype(BF16)
        scale_x[s, whole] = wide
        normed[s, whole] = xn
        qkv = dot(xn, weights_in[s])
        q, k = qkv[:, :HEAD], qkv[:, HEAD : 2 * HEAD]
        v = qkv[:, 2 * HEAD :].astype(BF16)
        rq = lax.rsqrt(dot((q * q).astype(BF16), mean) + EPSILON)
        rk = lax.rsqrt(dot((k * k).astype(BF16), mean) + EPSILON)
        qn = (q * rq).astype(BF16)
        kn = (k * rk).astype(BF16)
        scale_q[s, whole] = rq * HEAD**-0.5
        scale_k[s, whole] = rk * HEAD**-0.5
        queries[s, whole] = qn
        near_k = jnp.concatenate([keys[s, span_of(base, SPAN)], kn], axis=0)
        near_v = jnp.concatenate([values[s, span_of(base, SPAN)], v], axis=0)
        keys[s, padded] = kn
        values[s, padded] = v
        scores = [dot_nt(cut(qn, b), cut(near_k, b, 2 * SPAN)) for b in range(blocks)]
        raised = [
            (jnp.exp2(scores[b] * (LOG2E * HEAD**-0.5)) * mask[c * blocks + b]).astype(BF16)
            for b in range(blocks)
        ]
        both = [
            dot(raised[b], jnp.concatenate([cut(near_v, b, 2 * SPAN), ones], axis=1))
            for b in range(blocks)
        ]
        inverse = [1.0 / both[b][:, HEAD:] for b in range(blocks)]
        for b in range(blocks):
            chances[s, c * blocks + b] = (raised[b].astype(F32) * inverse[b]).astype(BF16)
        o = jnp.concatenate([(both[b][:, :HEAD] * inverse[b]).astype(BF16) for b in range(blocks)], axis=0)
        mixed[s, whole] = o
        branch = dot(o, weights[s, 3]).astype(BF16)
        new = (x + branch.astype(F32)).astype(BF16)
        states[s + 1, whole] = new

        @pl.when(s < SECTIONS - 1)
        def _():
            wide_new = new.astype(F32)
            start1(i + chunks, packed((wide_new * wide_new).astype(BF16)))

        @pl.when((i >= 1) & (i <= (SECTIONS - 1) * chunks))
        def _():
            start2(i + chunks - 1)

        return 0

    lax.fori_loop(0, SECTIONS * chunks, forward, 0)

    offset = SECTIONS * chunks

    def backward(j, _):
        s, c = SECTIONS - 1 - j // chunks, chunks - 1 - j % chunks
        base = c * chunk
        whole = span_of(base, chunk)

        @pl.when(j < chunks)
        def _():
            cot[whole] = states[SECTIONS, whole] * valid[whole]

        @pl.when(j >= chunks)
        def _():
            along = spread(finish(offset + j - chunks) * (1.0 / width))
            wide = scale_x[s + 1, whole]
            pulled = grad_normed[whole].astype(F32) * gain_of(s + 1)
            unit = states[s + 1, whole].astype(F32) * wide
            cot[whole] = (cot[whole].astype(F32) + wide * (pulled - unit * along)).astype(BF16)

        @pl.when(c == chunks - 1)
        def _():
            carry[...] = jnp.zeros_like(carry)

        g = cot[whole]
        o = mixed[s, whole]
        gm = dot(g, weights_back[s, 3 * HEAD :]).astype(BF16)
        delta = dot((gm.astype(F32) * o.astype(F32)).astype(BF16), ones)
        near = span_of(base, chunk + SPAN)
        near_k, near_v = keys[s, near], values[s, near]
        qn = queries[s, whole]
        grad_share = [dot_nt(cut(gm, b), cut(near_v, b, 2 * SPAN)) for b in range(blocks)]
        share = [chances[s, c * blocks + b] for b in range(blocks)]
        grad_score = [
            (share[b].astype(F32) * (grad_share[b] - cut(delta, b))).astype(BF16) for b in range(blocks)
        ]
        unit_v = [dot_tn(share[b], cut(gm, b)) for b in range(blocks)]
        unit_q = [dot(grad_score[b], cut(near_k, b, 2 * SPAN)) for b in range(blocks)]
        unit_k = [dot_tn(grad_score[b], cut(qn, b)) for b in range(blocks)]
        late_k = [unit_k[b][:SPAN] for b in range(1, blocks)] + [carry[0]]
        late_v = [unit_v[b][:SPAN] for b in range(1, blocks)] + [carry[1]]
        all_k = jnp.concatenate([unit_k[b][SPAN:] + late_k[b] for b in range(blocks)], axis=0)
        dv = jnp.concatenate([(unit_v[b][SPAN:] + late_v[b]).astype(BF16) for b in range(blocks)], axis=0)
        carry[0] = unit_k[0][:SPAN]
        carry[1] = unit_v[0][:SPAN]
        all_q = jnp.concatenate(unit_q, axis=0)
        wide_q = qn.astype(F32)
        wide_k = near_k[SPAN:].astype(F32)
        along_q = dot((all_q * wide_q).astype(BF16), mean)
        along_k = dot((all_k * wide_k).astype(BF16), mean)
        dq = (scale_q[s, whole] * (all_q - wide_q * along_q)).astype(BF16)
        dk = (scale_k[s, whole] * (all_k - wide_k * along_k)).astype(BF16)
        joined = jnp.concatenate([dq, dk, dv], axis=1)
        xn = normed[s, whole]

        @pl.when(s > 0)
        def _():
            grad = dot(joined, weights_back[s, : 3 * HEAD]).astype(BF16)
            grad_normed[whole] = grad
            start1(offset + j, packed((grad.astype(F32) * xn.astype(F32)).astype(BF16)))

        sums[s, 3] += dot_tn(o, g)
        part = dot_tn(xn, joined)
        for m in range(3):
            sums[s, m] += part[:, m * HEAD : (m + 1) * HEAD]

        @pl.when(c == 0)
        def _():
            start_halves(s)

        @pl.when((j >= 1) & (j <= (SECTIONS - 1) * chunks))
        def _():
            start2(offset + j - 1)

        @pl.when((j >= chunks) & (j % chunks == 0))
        def _():
            start_chips(s + 1)

        return 0

    lax.fori_loop(0, SECTIONS * chunks, backward, 0)

    start_chips(0)
    own_sum()

    def drain(item, _):
        pltpu.make_async_copy(recv1.at[item], recv1.at[item], send1_sem.at[item]).wait()
        pltpu.make_async_copy(recv2.at[item], recv2.at[item], send2_sem.at[item]).wait()
        return 0

    lax.fori_loop(0, offset + (SECTIONS - 1) * chunks, drain, 0)

    def drain_grads(s, _):
        pltpu.make_async_copy(half_send.at[s], half_send.at[s], half_send_sem.at[s]).wait()
        here = (place == s) & (replica // 2 == core)

        @pl.when(here)
        def _():
            pltpu.make_async_copy(chip_send.at[s, 0], chip_send.at[s, 0], chip_send_sem.at[s]).wait()

        @pl.when(jnp.logical_not(here))
        def _():
            pltpu.make_async_copy(chip_send.at[s], chip_send.at[s], chip_send_sem.at[s]).wait()

        return 0

    lax.fori_loop(0, SECTIONS, drain_grads, 0)
    pltpu.make_async_copy(own_recv, own_recv, own_send_sem).wait()

    @pl.when(in_window)
    def _():
        def settle(o, _):
            pltpu.make_async_copy(piece(me), piece(me), in_send).wait()
            return 0

        lax.fori_loop(1, seq, settle, 0)


def local(inputs, weights, gains, doc_lengths):
    seq, pipe, dp = lax.axis_size("seq"), lax.axis_size("pipe"), lax.axis_size("dp")
    total = inputs.shape[2] * seq
    width = gains.shape[1]
    rows = total // 2 + 2 * SPAN
    chunks = 3 if rows % (3 * GROUP) == 0 else 2
    chunk = rows // chunks
    across = 4 if seq > 4 else 2
    down = seq // across
    items = (2 * SECTIONS - 1) * chunks
    cfg = dict(
        total=total,
        seq=seq,
        pipe=pipe,
        dp=dp,
        width=width,
        across=across,
        rows=rows,
        chunk=chunk,
        chunks=chunks,
    )
    scratch = [
        pltpu.VMEM((SECTIONS, 4, HEAD, HEAD), BF16),
        pltpu.VMEM((SECTIONS, HEAD), F32),
        pltpu.VMEM(doc_lengths.shape[1:], jnp.int32),
        pltpu.VMEM((SECTIONS, HEAD, 3 * HEAD), BF16),
        pltpu.VMEM((SECTIONS, 4 * HEAD, HEAD), BF16),
        pltpu.VMEM((SECTIONS + 1, rows, HEAD), BF16),
        pltpu.VMEM((SECTIONS, rows, HEAD), BF16),
        pltpu.VMEM((SECTIONS, rows, HEAD), BF16),
        pltpu.VMEM((SECTIONS, SPAN + rows, HEAD), BF16),
        pltpu.VMEM((SECTIONS, SPAN + rows, HEAD), BF16),
        pltpu.VMEM((SECTIONS, rows, HEAD), BF16),
        pltpu.VMEM((SECTIONS, rows // SPAN, SPAN, 2 * SPAN), BF16),
        pltpu.VMEM((SECTIONS, rows, HEAD), F32),
        pltpu.VMEM((SECTIONS, rows, HEAD), F32),
        pltpu.VMEM((SECTIONS, rows, HEAD), F32),
        pltpu.VMEM((rows // SPAN, SPAN, 2 * SPAN), F32),
        pltpu.VMEM((rows, HEAD), BF16),
        pltpu.VMEM((rows, HEAD), BF16),
        pltpu.VMEM((rows, HEAD), BF16),
        pltpu.VMEM((2, SPAN, HEAD), F32),
        pltpu.VMEM((SECTIONS, 4, HEAD, HEAD), F32),
        pltpu.VMEM((SECTIONS, 8, HEAD), F32),
        pltpu.VMEM((items, 8, HEAD), F32),
        pltpu.VMEM((items, across - 1, 8, HEAD), F32),
        pltpu.VMEM((items, 8, HEAD), F32),
        pltpu.VMEM((items, down - 1, 8, HEAD), F32),
        pltpu.VMEM((SECTIONS, 2, HEAD, HEAD), BF16),
        pltpu.VMEM((SECTIONS, 2, HEAD, HEAD), BF16),
        pltpu.VMEM((SECTIONS, 2, HEAD, HEAD), BF16),
        pltpu.VMEM((2 * dp, HEAD, HEAD), BF16),
        pltpu.VMEM((HEAD, HEAD), BF16),
        pltpu.VMEM((dp - 1, HEAD, HEAD), BF16),
        pltpu.SemaphoreType.DMA((3,)),
        pltpu.SemaphoreType.DMA,
        pltpu.SemaphoreType.DMA,
        pltpu.SemaphoreType.DMA((items,)),
        pltpu.SemaphoreType.DMA((items,)),
        pltpu.SemaphoreType.DMA((items,)),
        pltpu.SemaphoreType.DMA((items,)),
        pltpu.SemaphoreType.DMA((SECTIONS,)),
        pltpu.SemaphoreType.DMA((SECTIONS,)),
        pltpu.SemaphoreType.DMA((SECTIONS,)),
        pltpu.SemaphoreType.DMA,
        pltpu.SemaphoreType.DMA,
        pltpu.SemaphoreType.DMA,
    ]
    hbm = pl.BlockSpec(memory_space=pltpu.HBM)
    return pl.pallas_call(
        functools.partial(kernel, cfg),
        out_shape=jax.ShapeDtypeStruct((1, 1, 4, HEAD, HEAD), F32),
        in_specs=[hbm, hbm, hbm, hbm],
        out_specs=pl.BlockSpec(memory_space=pltpu.VMEM),
        scratch_shapes=scratch,
        compiler_params=pltpu.CompilerParams(
            collective_id=0, has_side_effects=True, vmem_limit_bytes=60 * 1024 * 1024
        ),
    )(inputs, weights, gains, doc_lengths)


def solution(mesh):
    placed = (
        P("dp", None, "seq", None),
        P(None, "seq", None, None, None),
        P(),
        P("dp", None, None),
    )
    return jax.shard_map(
        local,
        mesh=mesh,
        in_specs=placed,
        out_specs=P("pipe", "seq", None, None, None),
        check_vma=False,
    )
```

time: 239 us -> 121 us (0.51)
  waiting for transfers between devices: 99.9 us -> 0 us
  between operations: 13.4 us -> 0.01 us
    psum x1 -> x0, waiting for transfers between devices: 54.1 us -> none  [local(): return lax.psum(own, 'dp').astype(F32)[:, None]]
    reduce_scatter x1 -> x0, waiting for transfers between devices: 45.8 us -> none  [local(): own = lax.psum_scatter(grads, 'pipe', scatter_dimension=0, tiled=True)]
  transfers between devices with their start and end apart: 2 -> 0, of which waited for: 2 -> 0; matrix products, arithmetic and copies ran while one was open for 0% -> 0% of each run, Pallas kernels for 0% -> 0%
where the time goes in v2:
time: 121 us; the launch traced here: 120 us
  Pallas kernels  119 us (98%)
  local copies, waits for them, and re-layouts  1.67 us (1%)
    pallas_call x1, Pallas kernels, local(): pl.pallas_call(functools.partial(kernel, cfg), out_shape=jax.ShapeDtypeSt...  119 us

profile of v2, /device:TPU:6, one launch (start us, length us, event | category | flops | bytes accessed | tf_op | source)
XLA Modules:
  0.0 120.3 jit_solution(7100707506148107072)
XLA Ops:
  0.0 118.6 %shard_map.46 = f32[1,1,4,128,128]{4,3,2,1,0:T(8,128)} custom-call(bf16[1,2,64,4096]{3,2,1,0:T(8,128)(2,1)} %inputs_ref.1, bf16[4,1,4,128,128]{4,3,2,1,0:T(8,128)(2,1)} %weights_ref.1, f32[4,4096]{1,0:T(4,128)} %gains_ref.1, s32[1,2,48]{2,1,0:T(2,128)} %docs_ref.1), custom_call_target="tpu_custom_call" | custom-call | tf_op jit(solution)/shard_map/pallas_call | solution.py:559
  118.6 1.7 %copy.6 = f32[1,1,4,128,128]{4,3,2,1,0:T(8,128)} copy(f32[1,1,4,128,128]{4,3,2,1,0:T(8,128)} %shard_map.46) | data formatting | bytes 524288

commit v3 on v2

--- a/solution.py
+++ b/solution.py
@@ -54,14 +54,17 @@
     mask,
     valid,
     cot,
-    grad_normed,
+    base_cot,
     carry,
     sums,
     gain_rows,
-    send1,
-    recv1,
-    send2,
-    recv2,
+    tokens,
+    square_send,
+    square_recv,
+    raw,
+    current,
+    sent,
+    received,
     half_send,
     half_recv,
     chip_send,
@@ -71,10 +74,10 @@
     load_sem,
     in_send,
     in_recv,
-    send1_sem,
-    recv1_sem,
-    send2_sem,
-    recv2_sem,
+    square_send_sem,
+    square_recv_sem,
+    sent_sem,
+    received_sem,
     half_send_sem,
     half_recv_sem,
     chip_send_sem,
@@ -86,7 +89,7 @@
     rows, chunk, chunks = cfg["rows"], cfg["chunk"], cfg["chunks"]
     pipe, dp = cfg["pipe"], cfg["dp"]
     down = seq // across
-    groups, blocks = chunk // GROUP, chunk // SPAN
+    groups, blocks = -(-chunk // GROUP), chunk // SPAN
     all_blocks = rows // SPAN
     place, me, replica = lax.axis_index("pipe"), lax.axis_index("seq"), lax.axis_index("dp")
     micro, half = place // 2, place % 2
@@ -94,7 +97,12 @@
     chip = micro * dp + replica
     first_block = half * (seq - all_blocks)
     window = first_block * SPAN
-    my_x, my_y = me % across, me // across
+    my_x, my_y = me & (across - 1), me // across
+    offsets = [(x, y) for y in range(down) for x in range(across)][1:]
+    offsets.sort(key=lambda o: -(min(o[0], across - o[0]) + min(o[1], down - o[1])))
+
+    def peer_at(offset):
+        return ((my_y + offset[1]) & (down - 1)) * across + ((my_x + offset[0]) & (across - 1))
 
     loads = [
         pltpu.make_async_copy(weights_ref.at[:, 0], weights, load_sem.at[0]),
@@ -102,48 +110,24 @@
             gains_ref.at[:, pl.ds(pl.multiple_of(me * HEAD, HEAD), HEAD)], gains, load_sem.at[1]
         ),
         pltpu.make_async_copy(docs_ref.at[0], docs, load_sem.at[2]),
+        pltpu.make_async_copy(inputs_ref.at[0, micro], tokens, load_sem.at[3]),
     ]
     for load in loads:
         load.start()
 
     barrier = pltpu.get_barrier_semaphore()
 
-    def greet(o, _):
-        pl.semaphore_signal(barrier, inc=1, device_id={"seq": (me + o) % seq})
-        return 0
-
-    def greet_column(o, _):
-        other = (place * dp + replica + o) % (pipe * dp)
+    for o in range(1, seq):
+        pl.semaphore_signal(barrier, inc=1, device_id={"seq": me ^ o})
+    for o in range(1, pipe * dp):
+        other = (place * dp + replica) ^ o
         pl.semaphore_signal(barrier, inc=1, device_id={"pipe": other // dp, "dp": other % dp})
-        return 0
-
-    lax.fori_loop(1, seq, greet, 0)
-    lax.fori_loop(1, pipe * dp, greet_column, 0)
-    pl.semaphore_wait(barrier, seq - 1 + pipe * dp - 1)
 
     slot = me - first_block
     in_window = (slot >= 0) & (slot < all_blocks)
 
     def piece(head):
-        return inputs_ref.at[0, micro, :, pl.ds(pl.multiple_of(head * HEAD, HEAD), HEAD)]
-
-    @pl.when(in_window)
-    def _():
-        landing = states.at[0, pl.ds(pl.multiple_of(slot * SPAN, SPAN), SPAN)]
-
-        def send(o, _):
-            peer = (me + o) % seq
-            pltpu.make_async_remote_copy(
-                src_ref=piece(peer),
-                dst_ref=landing,
-                send_sem=in_send,
-                recv_sem=in_recv,
-                device_id={"seq": peer},
-            ).start()
-            return 0
-
-        lax.fori_loop(1, seq, send, 0)
-        pltpu.make_async_copy(piece(me), landing, in_recv).start()
+        return tokens.at[:, pl.ds(pl.multiple_of(head * HEAD, HEAD), HEAD)]
 
     ones = jnp.full((HEAD, HEAD), 1.0, BF16)
     mean = jnp.full((HEAD, HEAD), 1.0 / HEAD, BF16)
@@ -183,6 +167,7 @@
         values[s, :SPAN] = jnp.zeros((SPAN, HEAD), BF16)
         gain_rows[s] = jnp.broadcast_to(gains[s : s + 1], (8, HEAD))
     sums[...] = jnp.zeros_like(sums)
+    current[...] = jnp.zeros_like(current)
 
     def arrange(s, _):
         for m in range(4):
@@ -194,7 +179,44 @@
 
     lax.fori_loop(0, SECTIONS, arrange, 0)
 
+    squares = jnp.zeros((SPAN, HEAD), F32)
+    for h in range(seq):
+        feature = tokens[:, h * HEAD : (h + 1) * HEAD].astype(F32)
+        squares = squares + feature * feature
+    twice = jnp.concatenate([squares, squares], axis=0)
+    high = twice.astype(BF16)
+    low = (twice - high.astype(F32)).astype(BF16)
+    square_send[...] = (dot_nt(ones[:8], high) + dot_nt(ones[:8], low))[:1]
+
+    pl.semaphore_wait(barrier, seq - 1 + pipe * dp - 1)
+
+    @pl.when(in_window)
+    def _():
+        landing = states.at[0, pl.ds(pl.multiple_of(slot * SPAN, SPAN), SPAN)]
+        for offset in offsets:
+            peer = peer_at(offset)
+            pltpu.make_async_remote_copy(
+                src_ref=piece(peer),
+                dst_ref=landing,
+                send_sem=in_send,
+                recv_sem=in_recv,
+                device_id={"seq": peer},
+            ).start()
+        pltpu.make_async_copy(piece(me), landing, in_recv).start()
+        for offset in offsets:
+            pltpu.make_async_remote_copy(
+                src_ref=square_send,
+                dst_ref=square_recv.at[slot],
+                send_sem=square_send_sem,
+                recv_sem=square_recv_sem,
+                device_id={"seq": peer_at(offset)},
+            ).start()
+        pltpu.make_async_copy(square_send, square_recv.at[slot], square_recv_sem).start()
+
     def packed(term):
+        if groups * GROUP > chunk:
+            spare = jnp.zeros((groups * GROUP - chunk, HEAD), BF16)
+            term = jnp.concatenate([term, spare], axis=0)
         total_rows = None
         for g in range(groups):
             pick = jnp.where(row8 == g, 1.0, 0.0).astype(BF16)
@@ -206,40 +228,27 @@
         high = packed_rows.astype(BF16)
         low = (packed_rows - high.astype(F32)).astype(BF16)
         wide = dot_tn(jnp.concatenate([high, low], axis=0), selector)
-        return jnp.concatenate([wide[:, g * HEAD : (g + 1) * HEAD] for g in range(groups)], axis=0)
-
-    def start1(item, part):
-        send1[item] = part
-        for o in range(1, across):
+        parts = [wide[:, g * HEAD : (g + 1) * HEAD] for g in range(groups)]
+        return jnp.concatenate(parts, axis=0)[:chunk]
+
+    def start(item, part):
+        sent[item] = part[:groups]
+        for n, offset in enumerate(offsets):
             pltpu.make_async_remote_copy(
-                src_ref=send1.at[item],
-                dst_ref=recv1.at[item, o - 1],
-                send_sem=send1_sem.at[item],
-                recv_sem=recv1_sem.at[item],
-                device_id={"seq": my_y * across + (my_x + o) % across},
+                src_ref=sent.at[item],
+                dst_ref=received.at[item, n],
+                send_sem=sent_sem.at[item],
+                recv_sem=received_sem.at[item],
+                device_id={"seq": peer_at(offset)},
             ).start()
 
-    def start2(item):
-        pltpu.make_async_copy(recv1.at[item], recv1.at[item], recv1_sem.at[item]).wait()
-        part = send1[item]
-        for o in range(across - 1):
-            part = part + recv1[item, o]
-        send2[item] = part
-        for o in range(1, down):
-            pltpu.make_async_remote_copy(
-                src_ref=send2.at[item],
-                dst_ref=recv2.at[item, o - 1],
-                send_sem=send2_sem.at[item],
-                recv_sem=recv2_sem.at[item],
-                device_id={"seq": ((my_y + o) % down) * across + my_x},
-            ).start()
-
     def finish(item):
-        pltpu.make_async_copy(recv2.at[item], recv2.at[item], recv2_sem.at[item]).wait()
-        part = send2[item]
-        for o in range(down - 1):
-            part = part + recv2[item, o]
-        return part
+        pltpu.make_async_copy(received.at[item], received.at[item], received_sem.at[item]).wait()
+        parts = [sent[item]] + [received[item, n] for n in range(seq - 1)]
+        while len(parts) > 1:
+            parts = [a + b for a, b in zip(parts[::2], parts[1::2])]
+        spare = jnp.zeros((8 - groups, HEAD), F32)
+        return jnp.concatenate([parts[0], spare], axis=0) if groups < 8 else parts[0]
 
     def span_of(start, size):
         return pl.ds(pl.multiple_of(start, SPAN), size)
@@ -304,41 +313,50 @@
         for o in range(1, dp):
             grads_ref[0, 0, (replica - o + dp) % dp] = own_recv[o - 1].astype(F32)
 
+    def project(s, c, x):
+        qkv = dot((x * gain_of(s)).astype(BF16), weights_in[s])
+        q, k = qkv[:, :HEAD], qkv[:, HEAD : 2 * HEAD]
+        raw[c, 0], raw[c, 1], raw[c, 2] = q, k, qkv[:, 2 * HEAD :]
+        raw[c, 3] = dot((q * q).astype(BF16), mean)
+        raw[c, 4] = dot((k * k).astype(BF16), mean)
+
     pltpu.make_async_copy(states.at[0], states.at[0], in_recv).wait()
 
     def begin(c, _):
-        x = states[0, span_of(c * chunk, chunk)].astype(F32)
-        start1(c, packed((x * x).astype(BF16)))
+        project(0, c, states[0, span_of(c * chunk, chunk)].astype(F32))
         return 0
 
     lax.fori_loop(0, chunks, begin, 0)
-    lax.fori_loop(0, chunks, lambda c, _: (start2(c), 0)[1], 0)
+    pltpu.make_async_copy(square_recv, square_recv, square_recv_sem).wait()
 
     def forward(i, _):
         s, c = i // chunks, i % chunks
         base = c * chunk
         whole = span_of(base, chunk)
         padded = span_of(base + SPAN, chunk)
-        rs = lax.rsqrt(finish(i) * (1.0 / width) + EPSILON)
-        wide = spread(rs)
+
+        @pl.when(i < chunks)
+        def _():
+            left = lax.broadcasted_iota(jnp.int32, (1, HEAD), 1) < SPAN
+            for g in range(groups):
+                first = c * blocks + 2 * g
+                second = c * blocks + min(2 * g + 1, blocks - 1)
+                current[g : g + 1] = jnp.where(left, square_recv[first], square_recv[second])
+
+        @pl.when(i >= chunks)
+        def _():
+            current[...] = finish(i - chunks)
+
+        wide = spread(lax.rsqrt(current[...] * (1.0 / width) + EPSILON))
+        squared = wide * wide
         x = states[s, whole].astype(F32)
-        xn = (x * wide * gain_of(s)).astype(BF16)
-        scale_x[s, whole] = wide
-        normed[s, whole] = xn
-        qkv = dot(xn, weights_in[s])
-        q, k = qkv[:, :HEAD], qkv[:, HEAD : 2 * HEAD]
-        v = qkv[:, 2 * HEAD :].astype(BF16)
-        rq = lax.rsqrt(dot((q * q).astype(BF16), mean) + EPSILON)
-        rk = lax.rsqrt(dot((k * k).astype(BF16), mean) + EPSILON)
-        qn = (q * rq).astype(BF16)
-        kn = (k * rk).astype(BF16)
-        scale_q[s, whole] = rq * HEAD**-0.5
-        scale_k[s, whole] = rk * HEAD**-0.5
-        queries[s, whole] = qn
+        rq = lax.rsqrt(squared * raw[c, 3] + EPSILON)
+        rk = lax.rsqrt(squared * raw[c, 4] + EPSILON)
+        qn = (raw[c, 0] * (wide * rq)).astype(BF16)
+        kn = (raw[c, 1] * (wide * rk)).astype(BF16)
+        v = (raw[c, 2] * wide).astype(BF16)
         near_k = jnp.concatenate([keys[s, span_of(base, SPAN)], kn], axis=0)
         near_v = jnp.concatenate([values[s, span_of(base, SPAN)], v], axis=0)
-        keys[s, padded] = kn
-        values[s, padded] = v
         scores = [dot_nt(cut(qn, b), cut(near_k, b, 2 * SPAN)) for b in range(blocks)]
         raised = [
             (jnp.exp2(scores[b] * (LOG2E * HEAD**-0.5)) * mask[c * blocks + b]).astype(BF16)
@@ -349,28 +367,32 @@
             for b in range(blocks)
         ]
         inverse = [1.0 / both[b][:, HEAD:] for b in range(blocks)]
+        o = jnp.concatenate([(both[b][:, :HEAD] * inverse[b]).astype(BF16) for b in range(blocks)], axis=0)
+        branch = dot(o, weights[s, 3]).astype(BF16)
+        new = (x + branch.astype(F32)).astype(BF16)
+        wide_new = new.astype(F32)
+        states[s + 1, whole] = new
+        scale_x[s, whole] = wide
+        scale_q[s, whole] = rq * HEAD**-0.5
+        scale_k[s, whole] = rk * HEAD**-0.5
+        queries[s, whole] = qn
+        keys[s, padded] = kn
+        values[s, padded] = v
+        mixed[s, whole] = o
         for b in range(blocks):
             chances[s, c * blocks + b] = (raised[b].astype(F32) * inverse[b]).astype(BF16)
-        o = jnp.concatenate([(both[b][:, :HEAD] * inverse[b]).astype(BF16) for b in range(blocks)], axis=0)
-        mixed[s, whole] = o
-        branch = dot(o, weights[s, 3]).astype(BF16)
-        new = (x + branch.astype(F32)).astype(BF16)
-        states[s + 1, whole] = new
 
         @pl.when(s < SECTIONS - 1)
         def _():
-            wide_new = new.astype(F32)
-            start1(i + chunks, packed((wide_new * wide_new).astype(BF16)))
-
-        @pl.when((i >= 1) & (i <= (SECTIONS - 1) * chunks))
-        def _():
-            start2(i + chunks - 1)
-
+            start(i, packed((wide_new * wide_new).astype(BF16)))
+            project(s + 1, c, wide_new)
+
+        normed[s, whole] = (x * wide * gain_of(s)).astype(BF16)
         return 0
 
     lax.fori_loop(0, SECTIONS * chunks, forward, 0)
 
-    offset = SECTIONS * chunks
+    later = (SECTIONS - 1) * chunks
 
     def backward(j, _):
         s, c = SECTIONS - 1 - j // chunks, chunks - 1 - j % chunks
@@ -383,11 +405,10 @@
 
         @pl.when(j >= chunks)
         def _():
-            along = spread(finish(offset + j - chunks) * (1.0 / width))
+            along = spread(finish(later + j - chunks) * (1.0 / width))
             wide = scale_x[s + 1, whole]
-            pulled = grad_normed[whole].astype(F32) * gain_of(s + 1)
-            unit = states[s + 1, whole].astype(F32) * wide
-            cot[whole] = (cot[whole].astype(F32) + wide * (pulled - unit * along)).astype(BF16)
+            unit = states[s + 1, whole].astype(F32) * (wide * wide)
+            cot[whole] = (base_cot[whole] - unit * along).astype(BF16)
 
         @pl.when(c == chunks - 1)
         def _():
@@ -410,26 +431,31 @@
         unit_k = [dot_tn(grad_score[b], cut(qn, b)) for b in range(blocks)]
         late_k = [unit_k[b][:SPAN] for b in range(1, blocks)] + [carry[0]]
         late_v = [unit_v[b][:SPAN] for b in range(1, blocks)] + [carry[1]]
+        all_v = jnp.concatenate([unit_v[b][SPAN:] + late_v[b] for b in range(blocks)], axis=0)
         all_k = jnp.concatenate([unit_k[b][SPAN:] + late_k[b] for b in range(blocks)], axis=0)
-        dv = jnp.concatenate([(unit_v[b][SPAN:] + late_v[b]).astype(BF16) for b in range(blocks)], axis=0)
+        dv = all_v.astype(BF16)
         carry[0] = unit_k[0][:SPAN]
         carry[1] = unit_v[0][:SPAN]
         all_q = jnp.concatenate(unit_q, axis=0)
         wide_q = qn.astype(F32)
         wide_k = near_k[SPAN:].astype(F32)
-        along_q = dot((all_q * wide_q).astype(BF16), mean)
-        along_k = dot((all_k * wide_k).astype(BF16), mean)
-        dq = (scale_q[s, whole] * (all_q - wide_q * along_q)).astype(BF16)
-        dk = (scale_k[s, whole] * (all_k - wide_k * along_k)).astype(BF16)
+        terms_q = all_q * wide_q
+        terms_k = all_k * wide_k
+        sq, sk = scale_q[s, whole], scale_k[s, whole]
+
+        @pl.when(s > 0)
+        def _():
+            small = (EPSILON * HEAD**0.5) * (sq * sq * terms_q + sk * sk * terms_k)
+            start(later + j, packed((all_v * near_v[SPAN:].astype(F32) + small).astype(BF16)))
+
+        along_q = dot(terms_q.astype(BF16), mean)
+        along_k = dot(terms_k.astype(BF16), mean)
+        dq = (sq * (all_q - wide_q * along_q)).astype(BF16)
+        dk = (sk * (all_k - wide_k * along_k)).astype(BF16)
         joined = jnp.concatenate([dq, dk, dv], axis=1)
         xn = normed[s, whole]
-
-        @pl.when(s > 0)
-        def _():
-            grad = dot(joined, weights_back[s, : 3 * HEAD]).astype(BF16)
-            grad_normed[whole] = grad
-            start1(offset + j, packed((grad.astype(F32) * xn.astype(F32)).astype(BF16)))
-
+        grad = dot(joined, weights_back[s, : 3 * HEAD]).astype(BF16)
+        base_cot[whole] = g.astype(F32) + scale_x[s, whole] * (grad.astype(F32) * gain_of(s))
         sums[s, 3] += dot_tn(o, g)
         part = dot_tn(xn, joined)
         for m in range(3):
@@ -439,10 +465,6 @@
         def _():
             start_halves(s)
 
-        @pl.when((j >= 1) & (j <= (SECTIONS - 1) * chunks))
-        def _():
-            start2(offset + j - 1)
-
         @pl.when((j >= chunks) & (j % chunks == 0))
         def _():
             start_chips(s + 1)
@@ -455,11 +477,10 @@
     own_sum()
 
     def drain(item, _):
-        pltpu.make_async_copy(recv1.at[item], recv1.at[item], send1_sem.at[item]).wait()
-        pltpu.make_async_copy(recv2.at[item], recv2.at[item], send2_sem.at[item]).wait()
+        pltpu.make_async_copy(received.at[item], received.at[item], sent_sem.at[item]).wait()
         return 0
 
-    lax.fori_loop(0, offset + (SECTIONS - 1) * chunks, drain, 0)
+    lax.fori_loop(0, 2 * later, drain, 0)
 
     def drain_grads(s, _):
         pltpu.make_async_copy(half_send.at[s], half_send.at[s], half_send_sem.at[s]).wait()
@@ -482,6 +503,7 @@
     def _():
         def settle(o, _):
             pltpu.make_async_copy(piece(me), piece(me), in_send).wait()
+            pltpu.make_async_copy(square_send, square_send, square_send_sem).wait()
             return 0
 
         lax.fori_loop(1, seq, settle, 0)
@@ -492,11 +514,12 @@
     total = inputs.shape[2] * seq
     width = gains.shape[1]
     rows = total // 2 + 2 * SPAN
-    chunks = 3 if rows % (3 * GROUP) == 0 else 2
+    chunks = 2
     chunk = rows // chunks
     across = 4 if seq > 4 else 2
     down = seq // across
-    items = (2 * SECTIONS - 1) * chunks
+    items = 2 * (SECTIONS - 1) * chunks
+    groups = -(-chunk // GROUP)
     cfg = dict(
         total=total,
         seq=seq,
@@ -527,25 +550,28 @@
         pltpu.VMEM((rows // SPAN, SPAN, 2 * SPAN), F32),
         pltpu.VMEM((rows, HEAD), BF16),
         pltpu.VMEM((rows, HEAD), BF16),
-        pltpu.VMEM((rows, HEAD), BF16),
+        pltpu.VMEM((rows, HEAD), F32),
         pltpu.VMEM((2, SPAN, HEAD), F32),
         pltpu.VMEM((SECTIONS, 4, HEAD, HEAD), F32),
         pltpu.VMEM((SECTIONS, 8, HEAD), F32),
-        pltpu.VMEM((items, 8, HEAD), F32),
-        pltpu.VMEM((items, across - 1, 8, HEAD), F32),
-        pltpu.VMEM((items, 8, HEAD), F32),
-        pltpu.VMEM((items, down - 1, 8, HEAD), F32),
+        pltpu.VMEM((SPAN, width), BF16),
+        pltpu.VMEM((1, HEAD), F32),
+        pltpu.VMEM((rows // SPAN, 1, HEAD), F32),
+        pltpu.VMEM((chunks, 5, chunk, HEAD), F32),
+        pltpu.VMEM((8, HEAD), F32),
+        pltpu.VMEM((items, groups, HEAD), F32),
+        pltpu.VMEM((items, seq - 1, groups, HEAD), F32),
         pltpu.VMEM((SECTIONS, 2, HEAD, HEAD), BF16),
         pltpu.VMEM((SECTIONS, 2, HEAD, HEAD), BF16),
         pltpu.VMEM((SECTIONS, 2, HEAD, HEAD), BF16),
         pltpu.VMEM((2 * dp, HEAD, HEAD), BF16),
         pltpu.VMEM((HEAD, HEAD), BF16),
         pltpu.VMEM((dp - 1, HEAD, HEAD), BF16),
-        pltpu.SemaphoreType.DMA((3,)),
+        pltpu.SemaphoreType.DMA((4,)),
         pltpu.SemaphoreType.DMA,
         pltpu.SemaphoreType.DMA,
-        pltpu.SemaphoreType.DMA((items,)),
-        pltpu.SemaphoreType.DMA((items,)),
+        pltpu.SemaphoreType.DMA,
+        pltpu.SemaphoreType.DMA,
         pltpu.SemaphoreType.DMA((items,)),
         pltpu.SemaphoreType.DMA((items,)),
         pltpu.SemaphoreType.DMA((SECTIONS,)),

time: 121 us -> 89.8 us (0.74)
  Pallas kernels: 119 us -> 87.7 us
    pallas_call x1, Pallas kernels: 119 us -> 87.7 us  [local(): pl.pallas_call(functools.partial(kernel, cfg), out_shape=jax.ShapeDtypeSt...]
where the time goes in v3:
time: 89.8 us; the launch traced here: 89.4 us
  Pallas kernels  87.7 us (98%)
  local copies, waits for them, and re-layouts  1.67 us (2%)
    pallas_call x1, Pallas kernels, local(): pl.pallas_call(functools.partial(kernel, cfg), out_shape=jax.ShapeDtypeSt...  87.7 us

profile of v3, /device:TPU:6, one launch (start us, length us, event | category | flops | bytes accessed | tf_op | source)
XLA Modules:
  0.0 89.4 jit_solution(11726442563999897524)
XLA Ops:
  0.0 87.7 %shard_map.46 = f32[1,1,4,128,128]{4,3,2,1,0:T(8,128)} custom-call(bf16[1,2,64,4096]{3,2,1,0:T(8,128)(2,1)} %inputs_ref.1, bf16[4,1,4,128,128]{4,3,2,1,0:T(8,128)(2,1)} %weights_ref.1, f32[4,4096]{1,0:T(4,128)} %gains_ref.1, s32[1,2,48]{2,1,0:T(2,128)} %docs_ref.1), custom_call_target="tpu_custom_call" | custom-call | tf_op jit(solution)/shard_map/pallas_call | solution.py:585
  87.7 1.7 %copy.6 = f32[1,1,4,128,128]{4,3,2,1,0:T(8,128)} copy(f32[1,1,4,128,128]{4,3,2,1,0:T(8,128)} %shard_map.46) | data formatting | bytes 524288

commit v4 on v3

--- a/solution.py
+++ b/solution.py
@@ -8,6 +8,7 @@
 from jax.sharding import PartitionSpec as P
 
 EPSILON = 1e-06
+EXTRA = 16
 SECTIONS = 4
 SPAN = 64
 HEAD = 128
@@ -59,8 +60,7 @@
     sums,
     gain_rows,
     tokens,
-    square_send,
-    square_recv,
+    landing,
     raw,
     current,
     sent,
@@ -74,8 +74,6 @@
     load_sem,
     in_send,
     in_recv,
-    square_send_sem,
-    square_recv_sem,
     sent_sem,
     received_sem,
     half_send_sem,
@@ -92,12 +90,12 @@
     groups, blocks = -(-chunk // GROUP), chunk // SPAN
     all_blocks = rows // SPAN
     place, me, replica = lax.axis_index("pipe"), lax.axis_index("seq"), lax.axis_index("dp")
-    micro, half = place // 2, place % 2
+    micro, half = place >> 1, place & 1
     core = half
     chip = micro * dp + replica
     first_block = half * (seq - all_blocks)
     window = first_block * SPAN
-    my_x, my_y = me & (across - 1), me // across
+    my_x, my_y = me & (across - 1), me >> (across.bit_length() - 1)
     offsets = [(x, y) for y in range(down) for x in range(across)][1:]
     offsets.sort(key=lambda o: -(min(o[0], across - o[0]) + min(o[1], down - o[1])))
 
@@ -110,25 +108,35 @@
             gains_ref.at[:, pl.ds(pl.multiple_of(me * HEAD, HEAD), HEAD)], gains, load_sem.at[1]
         ),
         pltpu.make_async_copy(docs_ref.at[0], docs, load_sem.at[2]),
-        pltpu.make_async_copy(inputs_ref.at[0, micro], tokens, load_sem.at[3]),
+        pltpu.make_async_copy(inputs_ref.at[0, micro], tokens.at[pl.ds(0, SPAN)], load_sem.at[3]),
     ]
     for load in loads:
         load.start()
 
     barrier = pltpu.get_barrier_semaphore()
 
-    for o in range(1, seq):
-        pl.semaphore_signal(barrier, inc=1, device_id={"seq": me ^ o})
-    for o in range(1, pipe * dp):
-        other = (place * dp + replica) ^ o
-        pl.semaphore_signal(barrier, inc=1, device_id={"pipe": other // dp, "dp": other % dp})
+    distant = [o for o in offsets if min(o[0], across - o[0]) + min(o[1], down - o[1]) > 3]
+    close = offsets[len(distant) :]
+    for offset in distant:
+        pl.semaphore_signal(barrier, inc=1, device_id={"seq": peer_at(offset)})
+    for q in range(pipe):
+        for r in range(dp):
+            if q or r:
+                there = {"pipe": place ^ q, "dp": replica ^ r}
+                pl.semaphore_signal(barrier, inc=1, device_id=there)
+    for offset in close:
+        pl.semaphore_signal(barrier, inc=1, device_id={"seq": peer_at(offset)})
 
     slot = me - first_block
-    in_window = (slot >= 0) & (slot < all_blocks)
+    own_blocks = seq // 2
+    lead = all_blocks - own_blocks
+    in_window = (slot >= half * lead) & (slot < own_blocks + 1 + half * (all_blocks - own_blocks - 1))
+    part = jnp.where(slot >= blocks, 1, 0)
 
     def piece(head):
         return tokens.at[:, pl.ds(pl.multiple_of(head * HEAD, HEAD), HEAD)]
 
+    later = (SECTIONS - 1) * chunks
     ones = jnp.full((HEAD, HEAD), 1.0, BF16)
     mean = jnp.full((HEAD, HEAD), 1.0 / HEAD, BF16)
     row8 = lax.broadcasted_iota(jnp.int32, (8, HEAD), 0)
@@ -148,70 +156,85 @@
     starts = dot(jnp.broadcast_to(lengths, (8, count)), jnp.where(earlier, 1.0, 0.0).astype(BF16))[:1]
     mid = total // 2
 
-    def make_mask(b, _):
-        base = window + b * SPAN
-        token = base + lax.broadcasted_iota(jnp.int32, (SPAN, HEAD), 0)
-        key = base - SPAN + lax.broadcasted_iota(jnp.int32, (SPAN, HEAD), 1)
-        reach = jnp.where(starts <= token.astype(F32), starts, 0.0)
-        begin = jnp.max(reach, axis=1, keepdims=True)
-        allowed = (key.astype(F32) >= begin) & (key <= token)
-        mask[b] = jnp.where(allowed, 1.0, 0.0)
-        late = jnp.where(begin >= mid, 1.0, 0.0)
-        mine = jnp.where(half == 1, late, 1.0 - late)
-        valid[pl.ds(pl.multiple_of(b * SPAN, SPAN), SPAN)] = jnp.broadcast_to(mine, (SPAN, HEAD)).astype(BF16)
-        return 0
-
-    lax.fori_loop(0, all_blocks, make_mask, 0)
-    for s in range(SECTIONS):
-        keys[s, :SPAN] = jnp.zeros((SPAN, HEAD), BF16)
-        values[s, :SPAN] = jnp.zeros((SPAN, HEAD), BF16)
-        gain_rows[s] = jnp.broadcast_to(gains[s : s + 1], (8, HEAD))
-    sums[...] = jnp.zeros_like(sums)
-    current[...] = jnp.zeros_like(current)
-
-    def arrange(s, _):
-        for m in range(4):
-            block = weights[s, m]
-            if m < 3:
-                weights_in[s, :, m * HEAD : (m + 1) * HEAD] = block
-            weights_back[s, m * HEAD : (m + 1) * HEAD] = jnp.transpose(block.astype(F32)).astype(BF16)
-        return 0
-
-    lax.fori_loop(0, SECTIONS, arrange, 0)
+    def prepare():
+        def make_mask(b, _):
+            base = window + b * SPAN
+            token = base + lax.broadcasted_iota(jnp.int32, (SPAN, HEAD), 0)
+            key = base - SPAN + lax.broadcasted_iota(jnp.int32, (SPAN, HEAD), 1)
+            reach = jnp.where(starts <= token.astype(F32), starts, 0.0)
+            begin = jnp.max(reach, axis=1, keepdims=True)
+            allowed = (key.astype(F32) >= begin) & (key <= token)
+            mask[b] = jnp.where(allowed, 1.0, 0.0)
+            late = jnp.where(begin >= mid, 1.0, 0.0)
+            mine = jnp.where(half == 1, late, 1.0 - late)
+            valid[pl.ds(pl.multiple_of(b * SPAN, SPAN), SPAN)] = jnp.broadcast_to(mine, (SPAN, HEAD)).astype(BF16)
+            return 0
+
+        lax.fori_loop(0, all_blocks, make_mask, 0)
+        for s in range(SECTIONS):
+            keys[s, :SPAN] = jnp.zeros((SPAN, HEAD), BF16)
+            values[s, :SPAN] = jnp.zeros((SPAN, HEAD), BF16)
+            gain_rows[s] = jnp.broadcast_to(gains[s : s + 1], (8, HEAD))
+        sums[...] = jnp.zeros_like(sums)
+
+        @pl.when(half == 0)
+        def _():
+            landing[own_blocks + 1 :] = jnp.zeros((all_blocks - own_blocks - 1, SPAN + EXTRA, HEAD), BF16)
+
+        @pl.when(half == 1)
+        def _():
+            landing[:lead] = jnp.zeros((lead, SPAN + EXTRA, HEAD), BF16)
+
+        current[...] = jnp.zeros_like(current)
+
+        def arrange(s, _):
+            for m in range(4):
+                block = weights[s, m]
+                if m < 3:
+                    weights_in[s, :, m * HEAD : (m + 1) * HEAD] = block
+                weights_back[s, m * HEAD : (m + 1) * HEAD] = jnp.transpose(block.astype(F32)).astype(BF16)
+            return 0
+
+        lax.fori_loop(0, SECTIONS, arrange, 0)
 
     squares = jnp.zeros((SPAN, HEAD), F32)
     for h in range(seq):
-        feature = tokens[:, h * HEAD : (h + 1) * HEAD].astype(F32)
+        feature = tokens[:SPAN, h * HEAD : (h + 1) * HEAD].astype(F32)
         squares = squares + feature * feature
     twice = jnp.concatenate([squares, squares], axis=0)
     high = twice.astype(BF16)
     low = (twice - high.astype(F32)).astype(BF16)
-    square_send[...] = (dot_nt(ones[:8], high) + dot_nt(ones[:8], low))[:1]
+    sum_row = (dot_nt(ones[:8], high) + dot_nt(ones[:8], low))[:1]
+    high = sum_row.astype(BF16)
+    low = (sum_row - high.astype(F32)).astype(BF16)
+    extra = jnp.concatenate([high, low, jnp.zeros((EXTRA - 2, HEAD), BF16)], axis=0)
+    for h in range(seq):
+        tokens[SPAN:, h * HEAD : (h + 1) * HEAD] = extra
+
+    early = (part == 0) & in_window
+
+    @pl.when(early)
+    def _():
+        prepare()
 
     pl.semaphore_wait(barrier, seq - 1 + pipe * dp - 1)
+
+    @pl.when(jnp.logical_not(early))
+    def _():
+        prepare()
 
     @pl.when(in_window)
     def _():
-        landing = states.at[0, pl.ds(pl.multiple_of(slot * SPAN, SPAN), SPAN)]
         for offset in offsets:
             peer = peer_at(offset)
             pltpu.make_async_remote_copy(
                 src_ref=piece(peer),
-                dst_ref=landing,
+                dst_ref=landing.at[slot],
                 send_sem=in_send,
-                recv_sem=in_recv,
+                recv_sem=in_recv.at[part],
                 device_id={"seq": peer},
             ).start()
-        pltpu.make_async_copy(piece(me), landing, in_recv).start()
-        for offset in offsets:
-            pltpu.make_async_remote_copy(
-                src_ref=square_send,
-                dst_ref=square_recv.at[slot],
-                send_sem=square_send_sem,
-                recv_sem=square_recv_sem,
-                device_id={"seq": peer_at(offset)},
-            ).start()
-        pltpu.make_async_copy(square_send, square_recv.at[slot], square_recv_sem).start()
+        pltpu.make_async_copy(piece(me), landing.at[slot], in_recv.at[part]).start()
 
     def packed(term):
         if groups * GROUP > chunk:
@@ -293,6 +316,34 @@
                     recv_sem=chip_recv_sem,
                     device_id={"pipe": s, "dp": owner},
                 ).start()
+
+    def drain():
+        def drain_item(item, _):
+            pltpu.make_async_copy(received.at[item], received.at[item], sent_sem.at[item]).wait()
+            return 0
+
+        lax.fori_loop(0, 2 * later, drain_item, 0)
+
+        def drain_grads(s, _):
+            pltpu.make_async_copy(half_send.at[s], half_send.at[s], half_send_sem.at[s]).wait()
+            here = (place == s) & (replica // 2 == core)
+
+            @pl.when(here)
+            def _():
+                pltpu.make_async_copy(chip_send.at[s, 0], chip_send.at[s, 0], chip_send_sem.at[s]).wait()
+
+            @pl.when(jnp.logical_not(here))
+            def _():
+                pltpu.make_async_copy(chip_send.at[s], chip_send.at[s], chip_send_sem.at[s]).wait()
+
+            return 0
+
+        lax.fori_loop(0, SECTIONS, drain_grads, 0)
+
+        @pl.when(in_window)
+        def _():
+            all_sent = tokens.at[:, pl.ds(0, (seq - 1) * HEAD)]
+            pltpu.make_async_copy(all_sent, all_sent, in_send).wait()
 
     def own_sum():
         pltpu.make_async_copy(chip_recv, chip_recv, chip_recv_sem).wait()
@@ -308,10 +359,12 @@
                 recv_sem=own_recv_sem,
                 device_id={"dp": (replica + o) % dp},
             ).start()
-        grads_ref[0, 0, replica] = part
+        grads_ref[0, 0, replica] = own_send[...]
+        drain()
         pltpu.make_async_copy(own_recv, own_recv, own_recv_sem).wait()
         for o in range(1, dp):
-            grads_ref[0, 0, (replica - o + dp) % dp] = own_recv[o - 1].astype(F32)
+            grads_ref[0, 0, (replica - o + dp) % dp] = own_recv[o - 1]
+        pltpu.make_async_copy(own_recv, own_recv, own_send_sem).wait()
 
     def project(s, c, x):
         qkv = dot((x * gain_of(s)).astype(BF16), weights_in[s])
@@ -320,14 +373,15 @@
         raw[c, 3] = dot((q * q).astype(BF16), mean)
         raw[c, 4] = dot((k * k).astype(BF16), mean)
 
-    pltpu.make_async_copy(states.at[0], states.at[0], in_recv).wait()
-
-    def begin(c, _):
-        project(0, c, states[0, span_of(c * chunk, chunk)].astype(F32))
-        return 0
-
-    lax.fori_loop(0, chunks, begin, 0)
-    pltpu.make_async_copy(square_recv, square_recv, square_recv_sem).wait()
+    def arrived(c):
+        for h in range(2):
+            first = max(c * blocks, lead if h else 0)
+            last = min((c + 1) * blocks, all_blocks if h else own_blocks + 1)
+
+            @pl.when(half == h)
+            def _():
+                there = landing.at[pl.ds(first, last - first)]
+                pltpu.make_async_copy(there, there, in_recv.at[c]).wait()
 
     def forward(i, _):
         s, c = i // chunks, i % chunks
@@ -335,13 +389,23 @@
         whole = span_of(base, chunk)
         padded = span_of(base + SPAN, chunk)
 
+        for k in range(chunks):
+            @pl.when(i == k)
+            def _():
+                arrived(k)
+
         @pl.when(i < chunks)
         def _():
+            new = jnp.concatenate([landing[c * blocks + b, :SPAN] for b in range(blocks)], axis=0)
+            states[0, whole] = new
+            project(0, c, new.astype(F32))
             left = lax.broadcasted_iota(jnp.int32, (1, HEAD), 1) < SPAN
             for g in range(groups):
-                first = c * blocks + 2 * g
-                second = c * blocks + min(2 * g + 1, blocks - 1)
-                current[g : g + 1] = jnp.where(left, square_recv[first], square_recv[second])
+                pair = []
+                for b in (2 * g, min(2 * g + 1, blocks - 1)):
+                    two = landing[c * blocks + b, SPAN:].astype(F32)
+                    pair.append(two[:1] + two[1:2])
+                current[g : g + 1] = jnp.where(left, pair[0], pair[1])
 
         @pl.when(i >= chunks)
         def _():
@@ -373,26 +437,25 @@
         wide_new = new.astype(F32)
         states[s + 1, whole] = new
         scale_x[s, whole] = wide
-        scale_q[s, whole] = rq * HEAD**-0.5
-        scale_k[s, whole] = rk * HEAD**-0.5
         queries[s, whole] = qn
         keys[s, padded] = kn
         values[s, padded] = v
         mixed[s, whole] = o
+
+        @pl.when(s < SECTIONS - 1)
+        def _():
+            start(i, packed((wide_new * wide_new).astype(BF16)))
+            project(s + 1, c, wide_new)
+
+        scale_q[s, whole] = rq * HEAD**-0.5
+        scale_k[s, whole] = rk * HEAD**-0.5
         for b in range(blocks):
             chances[s, c * blocks + b] = (raised[b].astype(F32) * inverse[b]).astype(BF16)
-
-        @pl.when(s < SECTIONS - 1)
-        def _():
-            start(i, packed((wide_new * wide_new).astype(BF16)))
-            project(s + 1, c, wide_new)
-
         normed[s, whole] = (x * wide * gain_of(s)).astype(BF16)
         return 0
 
     lax.fori_loop(0, SECTIONS * chunks, forward, 0)
 
-    later = (SECTIONS - 1) * chunks
 
     def backward(j, _):
         s, c = SECTIONS - 1 - j // chunks, chunks - 1 - j % chunks
@@ -421,21 +484,23 @@
         near = span_of(base, chunk + SPAN)
         near_k, near_v = keys[s, near], values[s, near]
         qn = queries[s, whole]
+        share = [chances[s, c * blocks + b] for b in range(blocks)]
+        unit_v = [dot_tn(share[b], cut(gm, b)) for b in range(blocks)]
+        late_v = [unit_v[b][:SPAN] for b in range(1, blocks)] + [carry[1]]
+        carry[1] = unit_v[0][:SPAN]
+        all_v = jnp.concatenate([unit_v[b][SPAN:] + late_v[b] for b in range(blocks)], axis=0)
+        dv = all_v.astype(BF16)
+        xn = normed[s, whole]
+
         grad_share = [dot_nt(cut(gm, b), cut(near_v, b, 2 * SPAN)) for b in range(blocks)]
-        share = [chances[s, c * blocks + b] for b in range(blocks)]
         grad_score = [
             (share[b].astype(F32) * (grad_share[b] - cut(delta, b))).astype(BF16) for b in range(blocks)
         ]
-        unit_v = [dot_tn(share[b], cut(gm, b)) for b in range(blocks)]
         unit_q = [dot(grad_score[b], cut(near_k, b, 2 * SPAN)) for b in range(blocks)]
         unit_k = [dot_tn(grad_score[b], cut(qn, b)) for b in range(blocks)]
         late_k = [unit_k[b][:SPAN] for b in range(1, blocks)] + [carry[0]]
-        late_v = [unit_v[b][:SPAN] for b in range(1, blocks)] + [carry[1]]
-        all_v = jnp.concatenate([unit_v[b][SPAN:] + late_v[b] for b in range(blocks)], axis=0)
         all_k = jnp.concatenate([unit_k[b][SPAN:] + late_k[b] for b in range(blocks)], axis=0)
-        dv = all_v.astype(BF16)
         carry[0] = unit_k[0][:SPAN]
-        carry[1] = unit_v[0][:SPAN]
         all_q = jnp.concatenate(unit_q, axis=0)
         wide_q = qn.astype(F32)
         wide_k = near_k[SPAN:].astype(F32)
@@ -453,13 +518,20 @@
         dq = (sq * (all_q - wide_q * along_q)).astype(BF16)
         dk = (sk * (all_k - wide_k * along_k)).astype(BF16)
         joined = jnp.concatenate([dq, dk, dv], axis=1)
-        xn = normed[s, whole]
-        grad = dot(joined, weights_back[s, : 3 * HEAD]).astype(BF16)
-        base_cot[whole] = g.astype(F32) + scale_x[s, whole] * (grad.astype(F32) * gain_of(s))
-        sums[s, 3] += dot_tn(o, g)
-        part = dot_tn(xn, joined)
-        for m in range(3):
-            sums[s, m] += part[:, m * HEAD : (m + 1) * HEAD]
+
+        @pl.when(s > 0)
+        def _():
+            grad = dot(joined, weights_back[s, : 3 * HEAD]).astype(BF16)
+            base_cot[whole] = g.astype(F32) + scale_x[s, whole] * (grad.astype(F32) * gain_of(s))
+
+        both = dot_tn(xn, joined[:, : 2 * HEAD])
+        sums[s, 0] += both[:, :HEAD]
+        sums[s, 1] += both[:, HEAD:]
+
+        @pl.when(s >= 0)
+        def _():
+            sums[s, 2] += dot_tn(normed[s, whole], all_v.astype(BF16))
+            sums[s, 3] += dot_tn(mixed[s, whole], cot[whole])
 
         @pl.when(c == 0)
         def _():
@@ -475,38 +547,6 @@
 
     start_chips(0)
     own_sum()
-
-    def drain(item, _):
-        pltpu.make_async_copy(received.at[item], received.at[item], sent_sem.at[item]).wait()
-        return 0
-
-    lax.fori_loop(0, 2 * later, drain, 0)
-
-    def drain_grads(s, _):
-        pltpu.make_async_copy(half_send.at[s], half_send.at[s], half_send_sem.at[s]).wait()
-        here = (place == s) & (replica // 2 == core)
-
-        @pl.when(here)
-        def _():
-            pltpu.make_async_copy(chip_send.at[s, 0], chip_send.at[s, 0], chip_send_sem.at[s]).wait()
-
-        @pl.when(jnp.logical_not(here))
-        def _():
-            pltpu.make_async_copy(chip_send.at[s], chip_send.at[s], chip_send_sem.at[s]).wait()
-
-        return 0
-
-    lax.fori_loop(0, SECTIONS, drain_grads, 0)
-    pltpu.make_async_copy(own_recv, own_recv, own_send_sem).wait()
-
-    @pl.when(in_window)
-    def _():
-        def settle(o, _):
-            pltpu.make_async_copy(piece(me), piece(me), in_send).wait()
-            pltpu.make_async_copy(square_send, square_send, square_send_sem).wait()
-            return 0
-
-        lax.fori_loop(1, seq, settle, 0)
 
 
 def local(inputs, weights, gains, doc_lengths):
@@ -554,9 +594,8 @@
         pltpu.VMEM((2, SPAN, HEAD), F32),
         pltpu.VMEM((SECTIONS, 4, HEAD, HEAD), F32),
         pltpu.VMEM((SECTIONS, 8, HEAD), F32),
-        pltpu.VMEM((SPAN, width), BF16),
-        pltpu.VMEM((1, HEAD), F32),
-        pltpu.VMEM((rows // SPAN, 1, HEAD), F32),
+        pltpu.VMEM((SPAN + EXTRA, width), BF16),
+        pltpu.VMEM((rows // SPAN, SPAN + EXTRA, HEAD), BF16),
         pltpu.VMEM((chunks, 5, chunk, HEAD), F32),
         pltpu.VMEM((8, HEAD), F32),
         pltpu.VMEM((items, groups, HEAD), F32),
@@ -569,9 +608,7 @@
         pltpu.VMEM((dp - 1, HEAD, HEAD), BF16),
         pltpu.SemaphoreType.DMA((4,)),
         pltpu.SemaphoreType.DMA,
-        pltpu.SemaphoreType.DMA,
-        pltpu.SemaphoreType.DMA,
-        pltpu.SemaphoreType.DMA,
+        pltpu.SemaphoreType.DMA((chunks,)),
         pltpu.SemaphoreType.DMA((items,)),
         pltpu.SemaphoreType.DMA((items,)),
         pltpu.SemaphoreType.DMA((SECTIONS,)),
@@ -584,14 +621,14 @@
     hbm = pl.BlockSpec(memory_space=pltpu.HBM)
     return pl.pallas_call(
         functools.partial(kernel, cfg),
-        out_shape=jax.ShapeDtypeStruct((1, 1, 4, HEAD, HEAD), F32),
+        out_shape=jax.ShapeDtypeStruct((1, 1, 4, HEAD, HEAD), BF16),
         in_specs=[hbm, hbm, hbm, hbm],
         out_specs=pl.BlockSpec(memory_space=pltpu.VMEM),
         scratch_shapes=scratch,
         compiler_params=pltpu.CompilerParams(
             collective_id=0, has_side_effects=True, vmem_limit_bytes=60 * 1024 * 1024
         ),
-    )(inputs, weights, gains, doc_lengths)
+    )(inputs, weights, gains, doc_lengths).astype(F32)
 
 
 def solution(mesh):

time: 89.8 us -> 88.6 us (0.987)
  local copies, waits for them, and re-layouts: 1.67 us -> 0 us
  other arithmetic: 0 us -> 1.63 us
  Pallas kernels: 87.7 us -> 86.6 us
    unnamed x1 -> x0, local copies, waits for them, and re-layouts: 1.67 us -> none
    convert_element_type x0 -> x1, other arithmetic: none -> 1.63 us  [local(): return pl.pallas_call(functools.partial(kernel, cfg), out_shape=jax.Shape...]
    pallas_call x1, Pallas kernels: 87.7 us -> 86.6 us  [local(): pl.pallas_call(functools.partial(kernel, cfg), out_shape=jax.ShapeDtypeSt...]
where the time goes in v4:
time: 88.6 us; the launch traced here: 88.2 us
  Pallas kernels  86.6 us (98%)
  other arithmetic  1.63 us (2%)
    pallas_call x1, Pallas kernels, local(): pl.pallas_call(functools.partial(kernel, cfg), out_shape=jax.ShapeDtypeSt...  86.6 us

profile of v4, /device:TPU:6, one launch (start us, length us, event | category | flops | bytes accessed | tf_op | source)
XLA Modules:
  0.0 88.2 jit_solution(12375765340168141589)
XLA Ops:
  0.0 86.6 %shard_map.46 = bf16[1,1,4,128,128]{4,3,2,1,0:T(8,128)(2,1)} custom-call(bf16[1,2,64,4096]{3,2,1,0:T(8,128)(2,1)} %inputs_ref.1, bf16[4,1,4,128,128]{4,3,2,1,0:T(8,128)(2,1)} %weights_ref.1, f32[4,4096]{1,0:T(4,128)} %gains_ref.1, s32[1,2,48]{2,1,0:T(2,128)} %docs_ref.1), custom_call_target="tpu_custom_call" | custom-call | tf_op jit(solution)/shard_map/pallas_call | solution.py:622
  86.6 1.6 %convert_element_type.3 = f32[1,1,4,128,128]{4,3,2,1,0:T(8,128)} convert(bf16[1,1,4,128,128]{4,3,2,1,0:T(8,128)(2,1)} %shard_map.46) | non-fusion elementwise | flops 65536 | bytes 393216 | tf_op jit(solution)/shard_map/convert_element_type | solution.py:631

commit v5 on v4

--- a/solution.py
+++ b/solution.py
@@ -282,6 +282,9 @@
     def cut(value, b, size=SPAN):
         return value[b * SPAN : b * SPAN + size]
 
+    def half_rows(p):
+        return pl.ds(p * SPAN, SPAN)
+
     def start_halves(s):
         for m in range(2):
             theirs = jnp.where(core == 0, sums[s, 2 + m], sums[s, m])
@@ -299,23 +302,25 @@
         for m in range(2):
             ours = jnp.where(core == 0, sums[s, m], sums[s, 2 + m])
             chip_send[s, m] = (ours + half_recv[s, m].astype(F32)).astype(BF16)
-        for m in range(2):
-            owner = core * 2 + m
-            here = (place == s) & (replica == owner)
-
-            @pl.when(here)
-            def _():
-                pltpu.make_async_copy(chip_send.at[s, m], chip_recv.at[chip], chip_recv_sem).start()
-
-            @pl.when(jnp.logical_not(here))
-            def _():
-                pltpu.make_async_remote_copy(
-                    src_ref=chip_send.at[s, m],
-                    dst_ref=chip_recv.at[chip],
-                    send_sem=chip_send_sem.at[s],
-                    recv_sem=chip_recv_sem,
-                    device_id={"pipe": s, "dp": owner},
-                ).start()
+        for p in range(2):
+            for m in range(2):
+                owner = core * 2 + m
+                here = (place == s) & (replica == owner)
+                source, target = chip_send.at[s, m, half_rows(p)], chip_recv.at[chip, half_rows(p)]
+
+                @pl.when(here)
+                def _():
+                    pltpu.make_async_copy(source, target, chip_recv_sem.at[p]).start()
+
+                @pl.when(jnp.logical_not(here))
+                def _():
+                    pltpu.make_async_remote_copy(
+                        src_ref=source,
+                        dst_ref=target,
+                        send_sem=chip_send_sem.at[s],
+                        recv_sem=chip_recv_sem.at[p],
+                        device_id={"pipe": s, "dp": owner},
+                    ).start()
 
     def drain():
         def drain_item(item, _):
@@ -346,25 +351,33 @@
             pltpu.make_async_copy(all_sent, all_sent, in_send).wait()
 
     def own_sum():
-        pltpu.make_async_copy(chip_recv, chip_recv, chip_recv_sem).wait()
-        part = chip_recv[0].astype(F32)
-        for k in range(1, 2 * dp):
-            part = part + chip_recv[k].astype(F32)
-        own_send[...] = part.astype(BF16)
-        for o in range(1, dp):
-            pltpu.make_async_remote_copy(
-                src_ref=own_send,
-                dst_ref=own_recv.at[o - 1],
-                send_sem=own_send_sem,
-                recv_sem=own_recv_sem,
-                device_id={"dp": (replica + o) % dp},
-            ).start()
+        for p in range(2):
+            at = half_rows(p)
+            there = chip_recv.at[:, at]
+            pltpu.make_async_copy(there, there, chip_recv_sem.at[p]).wait()
+            part = chip_recv[0, at].astype(F32)
+            for k in range(1, 2 * dp):
+                part = part + chip_recv[k, at].astype(F32)
+            own_send[at] = part.astype(BF16)
+            for o in range(1, dp):
+                pltpu.make_async_remote_copy(
+                    src_ref=own_send.at[at],
+                    dst_ref=own_recv.at[o - 1, at],
+                    send_sem=own_send_sem.at[p],
+                    recv_sem=own_recv_sem.at[p],
+                    device_id={"dp": (replica + o) & (dp - 1)},
+                ).start()
         grads_ref[0, 0, replica] = own_send[...]
         drain()
-        pltpu.make_async_copy(own_recv, own_recv, own_recv_sem).wait()
-        for o in range(1, dp):
-            grads_ref[0, 0, (replica - o + dp) % dp] = own_recv[o - 1]
-        pltpu.make_async_copy(own_recv, own_recv, own_send_sem).wait()
+        for p in range(2):
+            at = half_rows(p)
+            there = own_recv.at[:, at]
+            pltpu.make_async_copy(there, there, own_recv_sem.at[p]).wait()
+            for o in range(1, dp):
+                grads_ref[0, 0, (replica - o) & (dp - 1), at] = own_recv[o - 1, at]
+        for p in range(2):
+            there = own_recv.at[:, half_rows(p)]
+            pltpu.make_async_copy(there, there, own_send_sem.at[p]).wait()
 
     def project(s, c, x):
         qkv = dot((x * gain_of(s)).astype(BF16), weights_in[s])
@@ -614,9 +627,9 @@
         pltpu.SemaphoreType.DMA((SECTIONS,)),
         pltpu.SemaphoreType.DMA((SECTIONS,)),
         pltpu.SemaphoreType.DMA((SECTIONS,)),
-        pltpu.SemaphoreType.DMA,
-        pltpu.SemaphoreType.DMA,
-        pltpu.SemaphoreType.DMA,
+        pltpu.SemaphoreType.DMA((2,)),
+        pltpu.SemaphoreType.DMA((2,)),
+        pltpu.SemaphoreType.DMA((2,)),
     ]
     hbm = pl.BlockSpec(memory_space=pltpu.HBM)
     return pl.pallas_call(

time: 88.6 us -> 88.4 us (level)
  no operation moved by 1% of the time
where the time goes in v5:
time: 88.4 us; the launch traced here: 88.1 us
  Pallas kernels  86.4 us (98%)
  other arithmetic  1.63 us (2%)
    pallas_call x1, Pallas kernels, local(): pl.pallas_call(functools.partial(kernel, cfg), out_shape=jax.ShapeDtypeSt...  86.4 us

profile of v5, /device:TPU:6, one launch (start us, length us, event | category | flops | bytes accessed | tf_op | source)
XLA Modules:
  0.0 88.1 jit_solution(12187367527802890442)
XLA Ops:
  0.0 86.4 %shard_map.46 = bf16[1,1,4,128,128]{4,3,2,1,0:T(8,128)(2,1)} custom-call(bf16[1,2,64,4096]{3,2,1,0:T(8,128)(2,1)} %inputs_ref.1, bf16[4,1,4,128,128]{4,3,2,1,0:T(8,128)(2,1)} %weights_ref.1, f32[4,4096]{1,0:T(4,128)} %gains_ref.1, s32[1,2,48]{2,1,0:T(2,128)} %docs_ref.1), custom_call_target="tpu_custom_call" | custom-call | tf_op jit(solution)/shard_map/pallas_call | solution.py:635
  86.4 1.6 %convert_element_type.3 = f32[1,1,4,128,128]{4,3,2,1,0:T(8,128)} convert(bf16[1,1,4,128,128]{4,3,2,1,0:T(8,128)(2,1)} %shard_map.46) | non-fusion elementwise | flops 65536 | bytes 393216 | tf_op jit(solution)/shard_map/convert_element_type | solution.py:644

commit v6 on v5

--- a/solution.py
+++ b/solution.py
@@ -164,7 +164,7 @@
             reach = jnp.where(starts <= token.astype(F32), starts, 0.0)
             begin = jnp.max(reach, axis=1, keepdims=True)
             allowed = (key.astype(F32) >= begin) & (key <= token)
-            mask[b] = jnp.where(allowed, 1.0, 0.0)
+            mask[b] = jnp.where(allowed, 1.0, 0.0).astype(BF16)
             late = jnp.where(begin >= mid, 1.0, 0.0)
             mine = jnp.where(half == 1, late, 1.0 - late)
             valid[pl.ds(pl.multiple_of(b * SPAN, SPAN), SPAN)] = jnp.broadcast_to(mine, (SPAN, HEAD)).astype(BF16)
@@ -436,7 +436,7 @@
         near_v = jnp.concatenate([values[s, span_of(base, SPAN)], v], axis=0)
         scores = [dot_nt(cut(qn, b), cut(near_k, b, 2 * SPAN)) for b in range(blocks)]
         raised = [
-            (jnp.exp2(scores[b] * (LOG2E * HEAD**-0.5)) * mask[c * blocks + b]).astype(BF16)
+            jnp.exp2(scores[b] * (LOG2E * HEAD**-0.5)).astype(BF16) * mask[c * blocks + b]
             for b in range(blocks)
         ]
         both = [
@@ -550,9 +550,9 @@
         def _():
             start_halves(s)
 
-        @pl.when((j >= chunks) & (j % chunks == 0))
-        def _():
-            start_chips(s + 1)
+        @pl.when((c == 0) & (s > 0))
+        def _():
+            start_chips(s)
 
         return 0
 
@@ -600,7 +600,7 @@
         pltpu.VMEM((SECTIONS, rows, HEAD), F32),
         pltpu.VMEM((SECTIONS, rows, HEAD), F32),
         pltpu.VMEM((SECTIONS, rows, HEAD), F32),
-        pltpu.VMEM((rows // SPAN, SPAN, 2 * SPAN), F32),
+        pltpu.VMEM((rows // SPAN, SPAN, 2 * SPAN), BF16),
         pltpu.VMEM((rows, HEAD), BF16),
         pltpu.VMEM((rows, HEAD), BF16),
         pltpu.VMEM((rows, HEAD), F32),

time: 88.4 us -> 88.3 us (level)
  no operation moved by 1% of the time
where the time goes in v6:
time: 88.3 us; the launch traced here: 87.9 us
  Pallas kernels  86.3 us (98%)
  other arithmetic  1.63 us (2%)
    pallas_call x1, Pallas kernels, local(): pl.pallas_call(functools.partial(kernel, cfg), out_shape=jax.ShapeDtypeSt...  86.3 us

profile of v6, /device:TPU:6, one launch (start us, length us, event | category | flops | bytes accessed | tf_op | source)
XLA Modules:
  0.0 87.9 jit_solution(1283412573880075806)
XLA Ops:
  0.0 86.3 %shard_map.46 = bf16[1,1,4,128,128]{4,3,2,1,0:T(8,128)(2,1)} custom-call(bf16[1,2,64,4096]{3,2,1,0:T(8,128)(2,1)} %inputs_ref.1, bf16[4,1,4,128,128]{4,3,2,1,0:T(8,128)(2,1)} %weights_ref.1, f32[4,4096]{1,0:T(4,128)} %gains_ref.1, s32[1,2,48]{2,1,0:T(2,128)} %docs_ref.1), custom_call_target="tpu_custom_call" | custom-call | tf_op jit(solution)/shard_map/pallas_call | solution.py:635
  86.3 1.6 %convert_element_type.3 = f32[1,1,4,128,128]{4,3,2,1,0:T(8,128)} convert(bf16[1,1,4,128,128]{4,3,2,1,0:T(8,128)(2,1)} %shard_map.46) | non-fusion elementwise | flops 65536 | bytes 393216 | tf_op jit(solution)/shard_map/convert_element_type | solution.py:644
